TPU v7x, 32 devices: a whole 2x2x4 slice. The times are simulated.
32 devices in a mesh: dp: 4 (over y, x), tensor: 8 (over z, core).
Axes of the slice: x: 2, y: 2, z: 4, core: 2. Of those that a mesh axis runs over, the one named last changes fastest.
Arguments:
- tokens: bfloat16 [8, 1024, 2048], P('dp', 'tensor'), may hold values from -6 to 6
- cotangent: bfloat16 [8, 1024, 2048], P('dp', 'tensor'), may hold values from -6 to 6
- segments: int32 [8, 1024], P('dp'), may hold values from 0 to 5, never falling along the last dimension, each value on 1 to 640 neighbouring positions
- valid_mask: int32 [8, 1024], P('dp'), may hold values 0 or 1
- norm_params: float32 [2, 2048], replicated, may hold values from 0.5 to 1.5
- norm_moments: float32 [2, 2, 2048], replicated, may hold values from 0.0001 to 0.01
- heads_weight: float32 [3, 2048, 2048], P(None, 'dp', 'tensor'), may hold values from -0.125 to 0.125
- heads_moments: float32 [2, 3, 2048, 2048], P(None, None, 'dp', 'tensor'), may hold values from 0.0001 to 0.01
- heads_bias: float32 [3, 2048], P(None, 'tensor'), may hold values from -3 to 3
- heads_bias_moments: float32 [2, 3, 2048], P(None, None, 'tensor'), may hold values from 0.0001 to 0.01
- merge_weight: float32 [2048, 2048], P('tensor', 'dp'), may hold values from -0.5 to 0.5
- merge_moments: float32 [2, 2048, 2048], P(None, 'tensor', 'dp'), may hold values from 0.0001 to 0.01
- expand_weight: float32 [2048, 8192], P('dp', 'tensor'), may hold values from -0.125 to 0.125
- expand_moments: float32 [2, 2048, 8192], P(None, 'dp', 'tensor'), may hold values from 0.0001 to 0.01
- expand_bias: float32 [8192], P('tensor'), may hold values from -3 to 3
- expand_bias_moments: float32 [2, 8192], P(None, 'tensor'), may hold values from 0.0001 to 0.01
- shrink_weight: float32 [8192, 2048], P('tensor', 'dp'), may hold values from -0.0625 to 0.0625
- shrink_moments: float32 [2, 8192, 2048], P(None, 'tensor', 'dp'), may hold values from 0.0001 to 0.01
- output_bias: float32 [2, 2048], replicated, may hold values from -2 to 2
- output_bias_moments: float32 [2, 2, 2048], replicated, may hold values from 0.0001 to 0.01
Outputs:
- output: bfloat16 [8, 1024, 2048], P('dp', 'tensor')
- input_grad: bfloat16 [8, 1024, 2048], P('dp', 'tensor')
- norm_params_update: float32 [2, 2048], replicated
- norm_moments_new: float32 [2, 2, 2048], replicated
- heads_weight_update: float32 [3, 2048, 2048], P(None, 'dp', 'tensor')
- heads_moments_new: float32 [2, 3, 2048, 2048], P(None, None, 'dp', 'tensor')
- heads_bias_update: float32 [3, 2048], P(None, 'tensor')
- heads_bias_moments_new: float32 [2, 3, 2048], P(None, None, 'tensor')
- merge_weight_update: float32 [2048, 2048], P('tensor', 'dp')
- merge_moments_new: float32 [2, 2048, 2048], P(None, 'tensor', 'dp')
- expand_weight_update: float32 [2048, 8192], P('dp', 'tensor')
- expand_moments_new: float32 [2, 2048, 8192], P(None, 'dp', 'tensor')
- expand_bias_update: float32 [8192], P('tensor')
- expand_bias_moments_new: float32 [2, 8192], P(None, 'tensor')
- shrink_weight_update: float32 [8192, 2048], P('tensor', 'dp')
- shrink_moments_new: float32 [2, 8192, 2048], P(None, 'tensor', 'dp')
- output_bias_update: float32 [2, 2048], replicated
- output_bias_moments_new: float32 [2, 2, 2048], replicated
Inputs may be any that keep to these rules, and one draw needn't show every extreme that they name: In each sequence the segments numbers never fall; a document has at most 640 tokens, and one has exactly that many.
All inputs are finite; a program needn't handle non-finite values. No bound on the sum of `valid_mask` on one device may be relied on, other than what follows from the above.
Results may differ from a plain program's by a relative error of at most 0.02.
Values may be sent and summed in bfloat16 or wider, within the bound.
No kernel may reach another device: no remote copies, remote signals or barrier semaphores. Data moves between devices by JAX's collectives and lax.ppermute only.
A program may use at most 256 MiB of HBM per device.

v0:
```python
import math
from functools import partial

import jax
import jax.numpy as jnp
from jax import lax
from jax.experimental import pallas as pl
from jax.experimental.pallas import tpu as pltpu
from jax.sharding import PartitionSpec as P

HEAD_DIM = 64
ROT = 32
STEP = 5
LANES = 128

norm_eps = 1e-05
beta_first = 0.9
beta_second = 0.95
adam_eps = 1e-08
masked_score = -1000000000.0
score_scale = HEAD_DIM ** (-0.5)
VMEM = 60

f32 = jnp.float32
bf16 = jnp.bfloat16


def document_starts(segment):
    token_index = jnp.arange(segment.shape[0], dtype=jnp.int32)
    doc_begins = jnp.concatenate([jnp.ones((1,), dtype=jnp.bool_), segment[1:] != segment[:-1]])
    return lax.cummax(jnp.where(doc_begins, token_index, 0), axis=0)


def rotary_tables(doc_start):
    seq_len = doc_start.shape[0]
    positions = (jnp.arange(seq_len, dtype=jnp.int32) - doc_start).astype(f32)
    half_rot = ROT // 2
    frequency = jnp.power(10000.0, -2.0 * jnp.arange(half_rot, dtype=f32) / ROT)
    flat = jnp.zeros((HEAD_DIM - ROT,), f32)
    copies = LANES // HEAD_DIM
    by_lane = jnp.tile(jnp.concatenate([frequency, frequency, flat]), copies)
    sign = jnp.where(jnp.arange(LANES) % HEAD_DIM < half_rot, -1.0, 1.0)
    angles = positions[:, None] * by_lane[None, :]
    return jnp.cos(angles), jnp.sin(angles) * sign[None, :]


def masks(doc_start, valid):
    index = jnp.arange(doc_start.shape[0], dtype=jnp.int32)

    def build(query, start, key, key_valid):
        allowed = (key >= start) & (key <= query) & ((key_valid > 0) | (key == query))
        return jnp.where(allowed, 0.0, masked_score).astype(bf16)

    rows = build(index[:, None], doc_start[:, None], index[None, :], valid[None, :])
    columns = build(index[None, :], doc_start[None, :], index[:, None], valid[:, None])
    return rows, columns


def rotate(values, cosine, sine):
    half_rot = ROT // 2
    width = values.shape[1]
    lane = lax.broadcasted_iota(jnp.int32, values.shape, 1) % HEAD_DIM
    ahead = pltpu.roll(values, width - half_rot, 1)
    behind = pltpu.roll(values, half_rot, 1)
    partner = jnp.where(lane < half_rot, ahead, behind)
    return values * cosine + partner * sine


def nt(left, right):
    return lax.dot_general(left, right, (((1,), (1,)), ((), ())), preferred_element_type=f32)


def nn(left, right):
    return lax.dot_general(left, right, (((1,), (0,)), ((), ())), preferred_element_type=f32)


def tn(left, right):
    return lax.dot_general(left, right, (((0,), (0,)), ((), ())), preferred_element_type=f32)


def widen(table, width):
    return jnp.concatenate([table] * (width // LANES), axis=1)


one = pl.Buffered(1)


def resident(array):
    zeros = (0,) * array.ndim
    return pl.BlockSpec(array.shape, lambda *_: zeros, pipeline_mode=one)


def block_of(array, shape, place):
    return pl.BlockSpec(shape, lambda *_: place, pipeline_mode=one)


def staged(kernel, after, first, inputs, out_shape, name, grid, in_specs, out_specs, scratch_shapes=()):
    def without(first_ref, *refs):
        kernel(first_ref, *refs[len(after) :])

    return pl.pallas_call(
        without,
        grid_spec=pltpu.PrefetchScalarGridSpec(
            num_scalar_prefetch=1,
            grid=grid,
            in_specs=[*[pl.BlockSpec(memory_space=pl.ANY)] * len(after), *in_specs],
            out_specs=out_specs,
            scratch_shapes=scratch_shapes,
        ),
        out_shape=out_shape,
        compiler_params=pltpu.CompilerParams(vmem_limit_bytes=VMEM * 1024 * 1024),
        cost_estimate=pl.CostEstimate(flops=10**10, bytes_accessed=10**7, transcendentals=0),
        name=name,
    )(first, *after, *inputs)


def hold(arrays, after):
    def kernel(*refs):
        pass

    anywhere = pl.BlockSpec(memory_space=pl.ANY)
    return pl.pallas_call(
        kernel,
        in_specs=[anywhere] * (len(arrays) + len(after)),
        out_specs=[anywhere] * len(arrays),
        out_shape=[jax.ShapeDtypeStruct(array.shape, array.dtype) for array in arrays],
        input_output_aliases={at: at for at in range(len(arrays))},
        cost_estimate=pl.CostEstimate(flops=1000, bytes_accessed=1000, transcendentals=0),
        name="hold",
    )(*arrays, *after)


def attend_kernel(lows, first, low_ref, x_ref, bias_ref, cos_ref, sin_ref, mask_ref, *refs):
    *weights, qkv_ref, out_ref, lse_ref, k_all, v_all = refs
    seq, step = pl.program_id(0), pl.program_id(1)
    rows, width = out_ref.shape
    heads = width // HEAD_DIM
    blocks = k_all.shape[0] // rows
    cosine = widen(cos_ref[...], width)
    sine = widen(sin_ref[...], width)
    triple = []
    for which in range(3):
        total = None
        for low, ref in zip(lows, weights[which::3]):
            term = nn(x_ref[:, low : low + ref.shape[0]], ref[...])
            total = term if total is None else total + term
        triple.append(total + bias_ref[which : which + 1, :])
    query = rotate(triple[0], cosine, sine).astype(bf16)
    key = rotate(triple[1], cosine, sine).astype(bf16)
    value = triple[2].astype(bf16)
    qkv_ref[0] = query
    qkv_ref[1] = key
    qkv_ref[2] = value
    own = pl.ds(pl.multiple_of(step * rows, rows), rows)
    k_all[own, :] = key
    v_all[own, :] = value
    scaled = query * jnp.asarray(score_scale, bf16)
    head_of = lax.broadcasted_iota(jnp.int32, (rows, width), 1) // HEAD_DIM
    lane = lax.broadcasted_iota(jnp.int32, (rows, LANES), 1)
    span = step - low_ref[first + seq, step] + 1
    for count in range(1, blocks + 1):

        @pl.when(span == count)
        def _(count=count):
            begin = pl.multiple_of((step - (count - 1)) * rows, rows)
            keys = k_all[pl.ds(begin, count * rows), :]
            values = v_all[pl.ds(begin, count * rows), :]
            mask = mask_ref[:, pl.ds(begin, count * rows)].astype(f32)
            result = jnp.zeros((rows, width), f32)
            stats = jnp.zeros((rows, LANES), f32)
            for head in range(heads):
                mine = head_of == head
                scores = nt(jnp.where(mine, scaled, jnp.zeros_like(scaled)), keys) + mask
                top = jnp.max(scores, axis=1, keepdims=True)
                weights = jnp.exp(scores - top)
                total = jnp.sum(weights, axis=1, keepdims=True)
                mixed = nn(weights.astype(bf16), values) * (1.0 / total)
                result = jnp.where(mine, mixed, result)
                stats = jnp.where(lane == head, top + jnp.log(total), stats)
            out_ref[...] = result.astype(bf16)
            lse_ref[...] = jnp.transpose(stats)[: lse_ref.shape[0], :]


def attend(after, normed, first, count, entry, bias, cosine, sine, mask, low, rows):
    pieces, lows = entry
    _, seq_len, model_width = normed.shape
    width = bias.shape[1]
    blocks = seq_len // rows
    stat_rows = 8
    side = (pieces[0].shape[1] - 3 * width) // width

    def rows_of(columns):
        return pl.BlockSpec((None, rows, columns), lambda s, i, low: (first + s, i, 0))

    return staged(
        partial(attend_kernel, lows, first),
        after,
        low,
        [normed, bias, cosine, sine, mask, *[piece for piece in pieces for _ in range(3)]],
        [
            jax.ShapeDtypeStruct((3, count, seq_len, width), bf16),
            jax.ShapeDtypeStruct((count, seq_len, width), bf16),
            jax.ShapeDtypeStruct((count, stat_rows, seq_len), f32),
        ],
        "attend",
        grid=(count, blocks),
        in_specs=[
            rows_of(model_width),
            resident(bias),
            rows_of(LANES),
            rows_of(LANES),
            rows_of(seq_len),
            *[
                block_of(piece, (piece.shape[0], width), (0, side + which))
                for piece in pieces
                for which in range(3)
            ],
        ],
        out_specs=[
            pl.BlockSpec((3, None, rows, width), lambda s, i, low: (0, s, i, 0)),
            pl.BlockSpec((None, rows, width), lambda s, i, low: (s, i, 0)),
            pl.BlockSpec((None, stat_rows, rows), lambda s, i, low: (s, 0, i)),
        ],
        scratch_shapes=[pltpu.VMEM((seq_len, width), bf16), pltpu.VMEM((seq_len, width), bf16)],
    )


def attend_back_kernel(
    lows, first, low_ref, q_ref, k_ref, v_ref, o_ref, g_ref, lse_ref, mask_ref, cos_ref, sin_ref, *refs
):
    *weights, out_ref, sum_ref, dk_all, dv_all, k_turned = refs
    seq, step = pl.program_id(0), pl.program_id(1)
    rows, width = q_ref.shape
    heads = width // HEAD_DIM
    seq_len = dk_all.shape[0]
    blocks = seq_len // rows

    @pl.when(step == 0)
    def _():
        dk_all[...] = jnp.zeros_like(dk_all)
        dv_all[...] = jnp.zeros_like(dv_all)
        k_turned[...] = jnp.transpose(k_ref[...])

    @pl.when((step == 0) & (seq == 0))
    def _():
        sum_ref[...] = jnp.zeros_like(sum_ref)

    scaled = q_ref[...] * jnp.asarray(score_scale, bf16)
    d_out = None
    for low, ref in zip(lows, weights):
        term = nt(g_ref[:, low : low + ref.shape[1]], ref[...])
        d_out = term if d_out is None else d_out + term
    d_out = d_out.astype(bf16)
    zero = jnp.zeros_like(d_out)
    head_of = lax.broadcasted_iota(jnp.int32, (rows, width), 1) // HEAD_DIM
    product = d_out.astype(f32) * o_ref[...].astype(f32)
    high = product.astype(bf16)
    rest = (product - high.astype(f32)).astype(bf16)
    row_of = lax.broadcasted_iota(jnp.int32, (8, width), 0)
    by_head = (lax.broadcasted_iota(jnp.int32, (8, width), 1) // HEAD_DIM == row_of).astype(bf16)
    delta = nt(by_head, high) + nt(by_head, rest)
    own = pl.ds(pl.multiple_of(step * rows, rows), rows)
    span = step - low_ref[first + seq, step] + 1
    for count in range(1, blocks + 1):

        @pl.when(span == count)
        def _(count=count):
            begin = pl.multiple_of((step - (count - 1)) * rows, rows)
            reach = pl.ds(begin, count * rows)
            keys = k_ref[reach, :]
            values = v_ref[reach, :]
            mask = mask_ref[reach, :].astype(f32)
            probs_side, scores_side, queries_down, d_outs_down, d_query = [], [], [], [], []
            for head in range(heads):
                mine = head_of == head
                query = jnp.where(mine, scaled, zero)
                d_mine = jnp.where(mine, d_out, zero)
                scores = nt(keys, query) + mask
                probs = jnp.exp(scores - lse_ref[head : head + 1, :])
                d_probs = nt(values, d_mine)
                d_scores = (probs * (d_probs - delta[head : head + 1, :])).astype(bf16)
                d_query.append(nn(k_turned[head * HEAD_DIM : (head + 1) * HEAD_DIM, reach], d_scores))
                probs_side.append(probs.astype(bf16))
                scores_side.append(d_scores)
                queries_down.append(query)
                d_outs_down.append(d_mine)
            dv_all[reach, :] += nn(
                jnp.concatenate(probs_side, axis=1), jnp.concatenate(d_outs_down, axis=0)
            )
            dk_all[reach, :] += nn(
                jnp.concatenate(scores_side, axis=1), jnp.concatenate(queries_down, axis=0)
            )
            cosine = widen(cos_ref[own, :], width)
            sine = widen(sin_ref[own, :], width)
            d_rot = jnp.transpose(jnp.concatenate(d_query, axis=0)) * score_scale
            low_query = rotate(d_rot, cosine, -sine).astype(bf16)
            out_ref[own, :width] = low_query
            sum_ref[0:1, :] += jnp.sum(low_query.astype(f32), axis=0, keepdims=True)

    @pl.when(step == blocks - 1)
    def _():
        cosine = widen(cos_ref[...], width)
        sine = widen(sin_ref[...], width)
        low_key = rotate(dk_all[...], cosine, -sine).astype(bf16)
        low_value = dv_all[...].astype(bf16)
        out_ref[:, width : 2 * width] = low_key
        out_ref[:, 2 * width :] = low_value
        sum_ref[1:2, :] += jnp.sum(low_key.astype(f32), axis=0, keepdims=True)
        sum_ref[2:3, :] += jnp.sum(low_value.astype(f32), axis=0, keepdims=True)


def attend_back(after, qkv, attended, cot, first, count, exits, lse, mask, cosine, sine, low, rows):
    pieces, lows = exits
    _, seq_len, model_width = cot.shape
    width = qkv.shape[3]
    blocks = seq_len // rows
    stat_rows = lse.shape[1]
    units = pieces[0].shape[0] - width

    def whole_of(columns):
        return pl.BlockSpec((None, seq_len, columns), lambda s, i, low: (first + s, 0, 0))

    def rows_of(columns):
        return pl.BlockSpec((None, rows, columns), lambda s, i, low: (first + s, i, 0))

    return staged(
        partial(attend_back_kernel, lows, first),
        after,
        low,
        [qkv, qkv, qkv, attended, cot, lse, mask, cosine, sine, *pieces],
        [
            jax.ShapeDtypeStruct((count, seq_len, 3 * width), bf16),
            jax.ShapeDtypeStruct((8, width), f32),
        ],
        "attend_back",
        grid=(count, blocks),
        in_specs=[
            pl.BlockSpec((None, None, rows, width), lambda s, i, low: (0, first + s, i, 0)),
            pl.BlockSpec((None, None, seq_len, width), lambda s, i, low: (1, first + s, 0, 0)),
            pl.BlockSpec((None, None, seq_len, width), lambda s, i, low: (2, first + s, 0, 0)),
            rows_of(width),
            rows_of(model_width),
            pl.BlockSpec((None, stat_rows, rows), lambda s, i, low: (first + s, 0, i)),
            pl.BlockSpec((None, seq_len, rows), lambda s, i, low: (first + s, 0, i)),
            whole_of(LANES),
            whole_of(LANES),
            *[block_of(piece, (width, piece.shape[1]), (units // width, 0)) for piece in pieces],
        ],
        out_specs=[
            pl.BlockSpec((None, seq_len, 3 * width), lambda s, i, low: (s, 0, 0)),
            pl.BlockSpec((8, width), lambda s, i, low: (0, 0)),
        ],
        scratch_shapes=[
            pltpu.VMEM((seq_len, width), f32),
            pltpu.VMEM((seq_len, width), f32),
            pltpu.VMEM((width, seq_len), bf16),
        ],
    )


def gelu_kernel(lows, tick_ref, x_ref, bias_ref, *refs):
    *weights, hidden_ref, slope_ref = refs
    pre = bias_ref[...]
    for low, ref in zip(lows, weights):
        pre = pre + nn(x_ref[:, low : low + ref.shape[0]], ref[...])
    scale = (2.0 / math.pi) ** 0.5
    square = pre * pre
    half = 0.5 + 0.5 * jnp.tanh(pre * (scale + (scale * 0.044715) * square))
    hidden = pre * half
    hidden_ref[...] = hidden.astype(bf16)
    slope = half + hidden * (1.0 - half) * (2.0 * scale + (6.0 * scale * 0.044715) * square)
    slope_ref[...] = slope.astype(bf16)


def gelu_units(after, tick, normed, entry, bias, rows):
    pieces, lows = entry
    count, seq_len, model_width = normed.shape
    units = bias.shape[1]
    block = pl.BlockSpec((None, rows, units), lambda s, i, _: (s, i, 0))
    return staged(
        partial(gelu_kernel, lows),
        after,
        tick,
        [normed, bias, *pieces],
        [jax.ShapeDtypeStruct((count, seq_len, units), bf16)] * 2,
        "gelu_units",
        grid=(count, seq_len // rows),
        in_specs=[
                pl.BlockSpec((None, rows, model_width), lambda s, i, _: (s, i, 0)),
                resident(bias),
                *[block_of(piece, (piece.shape[0], units), (0, 0)) for piece in pieces],
            ],
        out_specs=[block, block],
    )


def out_kernel(lows, tick_ref, a_ref, h_ref, *refs):
    *weights, out_ref = refs
    units = h_ref.shape[1]
    for low, ref in zip(lows, weights):
        term = nn(h_ref[...], ref[:units, :]) + nn(a_ref[...], ref[units:, :])
        out_ref[:, low : low + ref.shape[1]] = term.astype(bf16)


def out_sums(after, tick, attended, hidden, exits, rows):
    pieces, lows = exits
    count, seq_len, width = attended.shape
    units = hidden.shape[2]
    model_width = sum(piece.shape[1] for piece in pieces)

    def rows_of(columns):
        return pl.BlockSpec((None, rows, columns), lambda s, i, _: (s, i, 0))

    return staged(
        partial(out_kernel, lows),
        after,
        tick,
        [attended, hidden, *pieces],
        jax.ShapeDtypeStruct((count, seq_len, model_width), bf16),
        "out_sums",
        grid=(count, seq_len // rows),
        in_specs=[rows_of(width), rows_of(units), *[resident(piece) for piece in pieces]],
        out_specs=rows_of(model_width),
    )


def back_rows_kernel(entry_lows, exit_lows, tick_ref, g_ref, slope_ref, c_ref, *refs):
    entry, exits = refs[: len(entry_lows)], refs[len(entry_lows) : len(entry_lows) + len(exit_lows)]
    hidden_ref, normed_ref, sum_ref = refs[-3:]
    units = slope_ref.shape[1]

    @pl.when((pl.program_id(0) == 0) & (pl.program_id(1) == 0))
    def _():
        sum_ref[...] = jnp.zeros_like(sum_ref)

    total = None
    for low, ref in zip(exit_lows, exits):
        term = nt(g_ref[:, low : low + ref.shape[1]], ref[...])
        total = term if total is None else total + term
    d_hidden = (total * slope_ref[...].astype(f32)).astype(bf16)
    hidden_ref[...] = d_hidden
    sum_ref[0:1, :] += jnp.sum(d_hidden.astype(f32), axis=0, keepdims=True)
    for low, ref in zip(entry_lows, entry):
        term = nt(d_hidden, ref[:, :units]) + nt(c_ref[...], ref[:, units:])
        normed_ref[:, low : low + ref.shape[0]] = term.astype(bf16)


def back_rows(after, tick, cot, slope, d_cat, entry, exits, rows):
    pieces, lows = entry
    exit_pieces, exit_lows = exits
    count, seq_len, model_width = cot.shape
    units = slope.shape[2]

    def rows_of(columns):
        return pl.BlockSpec((None, rows, columns), lambda s, i, _: (s, i, 0))

    return staged(
        partial(back_rows_kernel, lows, exit_lows),
        after,
        tick,
        [cot, slope, d_cat, *pieces, *exit_pieces],
        [
            jax.ShapeDtypeStruct((count, seq_len, units), bf16),
            jax.ShapeDtypeStruct((count, seq_len, model_width), bf16),
            jax.ShapeDtypeStruct((8, units), f32),
        ],
        "back_rows",
        grid=(count, seq_len // rows),
        in_specs=[
            rows_of(model_width),
            rows_of(units),
            rows_of(d_cat.shape[2]),
            *[resident(piece) for piece in pieces],
            *[block_of(piece, (units, piece.shape[1]), (0, 0)) for piece in exit_pieces],
        ],
        out_specs=[
            rows_of(units),
            rows_of(model_width),
            pl.BlockSpec((8, units), lambda s, i, _: (0, 0)),
        ],
    )


def targets(ranks, parts):
    if ranks == 4:
        half = parts // 2
        return [(0, half), (half, parts)] + [(at * parts, (at + 1) * parts) for at in range(1, ranks)]
    return [(at * parts, (at + 1) * parts) for at in range(ranks)]


def rows_grad_kernel(spans, tick_ref, left, right, *outs):
    step = pl.program_id(0)
    for (begin, end), out_ref in zip(spans, outs):

        @pl.when((step >= begin) & (step < end))
        def _(out_ref=out_ref):
            out_ref[...] = tn(left[...], right[...]).astype(bf16)


def rows_grad(after, tick, left, right, ranks, name):
    tokens, model_width = left.shape
    columns = right.shape[1]
    piece = model_width // ranks
    parts = max(2, piece // 256)
    block = piece // parts
    spans = targets(ranks, parts)

    def column_block(i, _):
        return (0, (ranks - 1 - i // parts) * parts + i % parts)

    def target_block(begin, end):
        return lambda i, _: (jnp.clip(i - begin, 0, end - begin - 1), 0)

    return staged(
        partial(rows_grad_kernel, spans),
        after,
        tick,
        [left, right],
        [jax.ShapeDtypeStruct(((end - begin) * block, columns), bf16) for begin, end in spans],
        name,
        grid=(ranks * parts,),
        in_specs=[pl.BlockSpec((tokens, block), column_block), resident(right)],
        out_specs=[pl.BlockSpec((block, columns), target_block(*span)) for span in spans],
    )


def columns_grad_kernel(spans, tick_ref, *refs):
    kinds = (len(refs) - 1 - len(spans)) // 2
    left, right, outs, turned = refs[:kinds], refs[kinds], refs[kinds + 1 : -kinds], refs[-kinds:]
    step = pl.program_id(0)

    @pl.when(step == 0)
    def _():
        for source, target in zip(left, turned):
            target[...] = jnp.transpose(source[...])

    for (begin, end), out_ref in zip(spans, outs):

        @pl.when((step >= begin) & (step < end))
        def _(out_ref=out_ref):
            first = 0
            for kind in range(kinds):
                total = nn(turned[kind][...], right[...])
                out_ref[first : first + total.shape[0], :] = total.astype(bf16)
                first += total.shape[0]


def columns_grad(after, tick, lefts, right, ranks, name):
    tokens, model_width = right.shape
    piece = model_width // ranks
    parts = 2
    block = piece // parts
    spans = targets(ranks, parts)
    height = sum(left.shape[1] for left in lefts)

    def column_block(i, _):
        return (0, (ranks - 1 - i // parts) * parts + i % parts)

    def target_block(begin, end):
        return lambda i, _: (0, jnp.clip(i - begin, 0, end - begin - 1))

    return staged(
        partial(columns_grad_kernel, spans),
        after,
        tick,
        [*lefts, right],
        [jax.ShapeDtypeStruct((height, (end - begin) * block), bf16) for begin, end in spans],
        name,
        grid=(ranks * parts,),
        in_specs=[*[resident(left) for left in lefts], pl.BlockSpec((tokens, block), column_block)],
        out_specs=[pl.BlockSpec((height, block), target_block(*span)) for span in spans],
        scratch_shapes=[pltpu.VMEM((left.shape[1], tokens), bf16) for left in lefts],
    )


def adam_step(moment_one, moment_two, gradient):
    moment_one = beta_first * moment_one + (1.0 - beta_first) * gradient
    moment_two = beta_second * moment_two + (1.0 - beta_second) * gradient * gradient
    first_fix = 1.0 - beta_first**STEP
    second_fix = 1.0 - beta_second**STEP
    update = moment_one / first_fix / (jnp.sqrt(moment_two / second_fix) + adam_eps)
    return update, moment_one, moment_two


def adam_update(moments, gradient):
    update, moment_one, moment_two = adam_step(moments[0], moments[1], gradient)
    return update, jnp.stack([moment_one, moment_two])


def adam_kernel(scale, tick_ref, moments_ref, *refs):
    *terms, update_ref, new_ref = refs
    gradient = terms[0][...].astype(f32)
    for term in terms[1:]:
        gradient = gradient + term[...].astype(f32)
    update, moment_one, moment_two = adam_step(moments_ref[0], moments_ref[1], gradient * scale)
    update_ref[...] = update
    new_ref[0] = moment_one
    new_ref[1] = moment_two


def adam_sum(after, tick, moments, terms, scale, row, column, parts):
    groups = parts if parts else 1
    height, width = moments.shape[-2:]
    rows = min(256, height)
    steps = height // rows
    if parts:
        moment_block = pl.BlockSpec((2, None, rows, width), lambda p, i, _: (0, p, i, 0))
        update_block = pl.BlockSpec((None, rows, width), lambda p, i, _: (p, i, 0))
    else:
        moment_block = pl.BlockSpec((2, rows, width), lambda p, i, _: (0, i, 0))
        update_block = pl.BlockSpec((rows, width), lambda p, i, _: (i, 0))
    term_block = pl.BlockSpec((rows, width), lambda p, i, _: (row // rows + i, column // width + p))
    return staged(
        partial(adam_kernel, scale),
        after,
        tick,
        [moments, *terms],
        [
            jax.ShapeDtypeStruct(moments.shape[1:], f32),
            jax.ShapeDtypeStruct(moments.shape, f32),
        ],
        "adam_sum",
        grid=(groups, steps),
        in_specs=[moment_block, *[term_block] * len(terms)],
        out_specs=[update_block, moment_block],
    )


def from_relative(ref, rank, ranks, piece):
    return jnp.concatenate(
        [ref[:, pl.ds(pl.multiple_of((rank ^ j) * piece, piece), piece)] for j in range(ranks)], axis=1
    )


def input_grad_kernel(ranks, rank_ref, x_ref, g_ref, norm_ref, d_ref, out_ref, sum_ref):
    piece = x_ref.shape[1] // ranks
    inputs = x_ref[...].astype(f32)
    centred = inputs - jnp.mean(inputs, axis=1, keepdims=True)
    variance = jnp.mean(centred * centred, axis=1, keepdims=True)
    inv_std = lax.rsqrt(variance + norm_eps)
    unit = centred * inv_std
    cot = g_ref[...].astype(f32)

    @pl.when(pl.program_id(0) == 0)
    def _():
        sum_ref[...] = jnp.zeros_like(sum_ref)

    d_normed = from_relative(d_ref, rank_ref[0], ranks, piece).astype(f32)
    d_unit = d_normed * norm_ref[0:1, :]
    mean_unit = jnp.mean(d_unit, axis=1, keepdims=True)
    mean_cross = jnp.mean(d_unit * unit, axis=1, keepdims=True)
    out_ref[...] = (cot + inv_std * (d_unit - mean_unit - unit * mean_cross)).astype(bf16)
    sum_ref[0:1, :] += jnp.sum(d_normed * unit, axis=0, keepdims=True)
    sum_ref[1:2, :] += jnp.sum(d_normed, axis=0, keepdims=True)
    sum_ref[2:3, :] += jnp.sum(cot, axis=0, keepdims=True)


def input_gradient(after, rank, tokens, cot_rows, norm_params, grads, ranks):
    count, rows, model_width = tokens.shape
    block = pl.BlockSpec((None, rows, model_width), lambda s, _: (s, 0, 0))
    return staged(
        partial(input_grad_kernel, ranks),
        after,
        rank,
        [tokens, cot_rows, norm_params, grads],
        [
            jax.ShapeDtypeStruct(tokens.shape, bf16),
            jax.ShapeDtypeStruct((8, model_width), f32),
        ],
        "input_grad",
        grid=(count,),
        in_specs=[block, block, resident(norm_params), block],
        out_specs=[block, pl.BlockSpec((8, model_width), lambda s, _: (0, 0))],
    )


def output_kernel(ranks, rank_ref, x_ref, bias_ref, o_ref, out_ref):
    piece = x_ref.shape[1] // ranks
    branches = from_relative(o_ref, rank_ref[0], ranks, piece).astype(f32)
    total = x_ref[...].astype(f32) + branches + bias_ref[0:1, :] + bias_ref[1:2, :]
    out_ref[...] = total.astype(bf16)


def layer_output(after, rank, tokens, output_bias, outs, ranks):
    count, rows, model_width = tokens.shape
    block = pl.BlockSpec((None, rows, model_width), lambda s, _: (s, 0, 0))
    return staged(
        partial(output_kernel, ranks),
        after,
        rank,
        [tokens, output_bias, outs],
        jax.ShapeDtypeStruct(tokens.shape, bf16),
        "layer_output",
        grid=(count,),
        in_specs=[block, resident(output_bias), block],
        out_specs=block,
    )


def swap(array, distance):
    size = lax.axis_size("dp")
    return lax.ppermute(array, "dp", [(i, i ^ distance) for i in range(size)])


def plus(left, right):
    return (left.astype(f32) + right.astype(f32)).astype(bf16)


class Line:
    def __init__(self, tick):
        self.tick, self.pending = tick, []

    def wait(self, *arrays):
        self.pending += arrays

    def run(self, stage, *arguments):
        result = stage(self.pending, *arguments)
        self.pending = [jax.tree.leaves(result)[0]]
        return result


class Gather:
    def __init__(self, own, axis):
        self.size = lax.axis_size("dp")
        self.own, self.axis = own, axis
        self.sent = [swap(own, j) for j in ((1, 2) if self.size == 4 else range(1, self.size))]
        self.rest = []

    def forward(self, after):
        if self.size == 4:
            if after:
                self.sent = hold(self.sent, after)
            half = self.own.shape[self.axis] // 2
            near, far = self.sent
            top = lax.slice_in_dim(near, 0, half, axis=self.axis)
            bottom = lax.slice_in_dim(far, half, 2 * half, axis=self.axis)
            self.rest = [swap(top, 2), swap(bottom, 1)]

    def pieces(self):
        pieces = [self.own, *self.sent, *self.rest]
        lows, low = [], 0
        for piece in pieces:
            lows.append(low)
            low += piece.shape[self.axis]
        return pieces, tuple(lows)


class Scatter:
    def __init__(self, pieces, axis, after=()):
        self.size = lax.axis_size("dp")
        self.axis = axis
        if self.size == 4:
            *ends, self.far, self.near, self.own = pieces
            top, bottom = hold(ends, after) if after else ends
            self.ends = [top, bottom]
            self.first = [swap(top, 1), swap(bottom, 2)]
        else:
            self.ends = []
            self.own = pieces[-1]
            self.first = [swap(piece, self.size - 1 - at) for at, piece in enumerate(pieces[:-1])]

    def forward(self, after=()):
        if self.size != 4:
            return [self.own, *self.first]
        top, bottom = hold(self.first, after) if after else self.first
        half = self.near.shape[self.axis] // 2

        def halves(array):
            return [lax.slice_in_dim(array, at, at + half, axis=self.axis) for at in (0, half)]

        near, far = halves(self.near), halves(self.far)
        near = jnp.concatenate([near[0], plus(near[1], bottom)], axis=self.axis)
        far = jnp.concatenate([plus(far[0], top), far[1]], axis=self.axis)
        return [self.own, swap(near, 1), swap(far, 2)]


def sum_axis(array, axis, distances):
    size = lax.axis_size(axis)
    offsets = [0]
    for distance in distances:
        offsets += [offset + distance for offset in offsets]
    terms = [lax.ppermute(array, axis, [(i, i ^ offset) for i in range(size)]) for offset in offsets[1:]]
    terms = [array, *terms]
    while len(terms) > 1:
        terms = [left + right for left, right in zip(terms[::2], terms[1::2])]
    return terms[0]


def sum_over(array, axis):
    distances = [1 << bit for bit in range((lax.axis_size(axis) - 1).bit_length())]
    first = len(distances) % 2
    if first:
        array = sum_axis(array, axis, distances[:1])
    for at in range(first, len(distances), 2):
        array = sum_axis(array, axis, distances[at : at + 2])
    return array


def body(
    tokens,
    cotangent,
    segments,
    valid_mask,
    norm_params,
    norm_moments,
    heads_weight,
    heads_moments,
    heads_bias,
    heads_bias_moments,
    merge_weight,
    merge_moments,
    expand_weight,
    expand_moments,
    expand_bias,
    expand_bias_moments,
    shrink_weight,
    shrink_moments,
    output_bias,
    output_bias_moments,
):
    ranks = lax.axis_size("dp")
    rank = lax.axis_index("dp")
    count, _, model_width = tokens.shape
    seq_len = segments.shape[1]
    width = heads_weight.shape[2]
    piece = model_width // ranks
    rows = min(256, seq_len)

    def relative(array):
        parts = [
            lax.dynamic_slice_in_dim(array, (rank ^ j) * piece, piece, array.ndim - 1) for j in range(ranks)
        ]
        return jnp.concatenate(parts, axis=-1)

    norm_rel = relative(norm_params)
    norm_gain, norm_shift = norm_rel[0], norm_rel[1]
    inputs = relative(tokens).astype(f32)
    cot_rows = relative(cotangent)
    row_mean = jnp.mean(inputs, axis=-1, keepdims=True)
    centred = inputs - row_mean
    variance = jnp.mean(centred * centred, axis=-1, keepdims=True)
    inv_std = lax.rsqrt(variance + norm_eps)
    unit = centred * inv_std
    normed_rows = (unit * norm_gain + norm_shift).astype(bf16)

    def gather_rows(array):
        return lax.all_gather(array, "tensor", axis=1, tiled=True)

    def scatter_rows(array):
        return lax.psum_scatter(array, "tensor", scatter_dimension=1, tiled=True)

    tick = segments[0, :1]
    line = Line(tick)
    rank_here = rank.reshape(1).astype(jnp.int32)
    normed = gather_rows(normed_rows)
    cot = gather_rows(cot_rows)

    entry_own = jnp.concatenate([expand_weight, *[heads_weight[c] for c in range(3)]], axis=1).astype(bf16)
    entry_gather = Gather(entry_own, 0)
    entry_gather.forward(())
    entry = entry_gather.pieces()
    exit_own = jnp.concatenate([shrink_weight, merge_weight], axis=0).astype(bf16)
    exit_gather = Gather(hold([exit_own], entry_gather.rest or entry_gather.sent)[0], 1)
    starts = jnp.stack([document_starts(segments[s]) for s in range(count)])
    cosine, sine = jax.vmap(rotary_tables)(starts)
    mask_rows, mask_columns = jax.vmap(masks)(starts, valid_mask)
    lows = starts[:, ::rows] // rows
    expand_row = expand_bias.reshape(1, -1)
    big = min(512, seq_len)
    units_local = expand_weight.shape[1]

    line.wait(mask_columns)
    qkv, attended, lse = line.run(
        attend, normed, 0, count, entry, heads_bias, cosine, sine, mask_rows, lows, rows
    )
    exit_gather.forward([attended])
    exits = exit_gather.pieces()
    hidden, slope = line.run(gelu_units, tick, normed, entry, expand_row, big)
    partials = line.run(out_sums, tick, attended, hidden, exits, big)

    outs = scatter_rows(partials)

    def tokens_of(array):
        return array.reshape(-1, array.shape[-1])

    def adam(moments, terms, row=0, column=0, parts=0):
        return line.run(adam_sum, tick, moments, terms, 1.0 / seq_len, row, column, parts)

    exit_parts = line.run(
        columns_grad, tick, [tokens_of(hidden), tokens_of(attended)], tokens_of(cot), ranks, "exit_grad"
    )
    exit_scatter = Scatter(exit_parts, 1)
    d_cat, bias_sums = line.run(
        attend_back, qkv, attended, cot, 0, count, exits, lse, mask_columns, cosine, sine, lows, rows
    )
    exit_terms = exit_scatter.forward([d_cat])
    d_hidden, sums, hidden_sums = line.run(back_rows, tick, cot, slope, d_cat, entry, exits, big)
    grads = scatter_rows(hold([sums], exit_terms[1:])[0])
    line.wait(outs)
    expand_parts = line.run(rows_grad, tick, tokens_of(normed), tokens_of(d_hidden), ranks, "expand_grad")
    expand_scatter = Scatter(expand_parts, 0)
    expand_terms = expand_scatter.forward()
    heads_parts = line.run(rows_grad, tick, tokens_of(normed), tokens_of(d_cat), ranks, "heads_grad")
    heads_scatter = Scatter(heads_parts, 0, expand_scatter.first)
    heads_terms = heads_scatter.forward()
    line.wait(*heads_scatter.ends)
    shrink_upd, shrink_mom = adam(shrink_moments, exit_terms)
    merge_upd, merge_mom = adam(merge_moments, exit_terms, row=units_local)
    line.wait(*heads_scatter.first)
    output = line.run(layer_output, rank_here, tokens, output_bias, outs, ranks)
    expand_upd, expand_mom = adam(expand_moments, expand_terms)
    line.wait(*heads_terms[1:])
    input_grad, column_sums = line.run(
        input_gradient, rank_here, tokens, cotangent, norm_params, grads, ranks
    )
    heads_upd, heads_mom = adam(heads_moments, heads_terms, parts=3)
    column_sums = sum_over(column_sums, "tensor")
    bias_sums = jnp.concatenate([bias_sums[:3].reshape(-1), hidden_sums[0]])
    totals = sum_over(jnp.concatenate([column_sums[:3].reshape(-1), bias_sums]), "dp")
    norm_total = totals[: 2 * model_width].reshape(2, model_width)
    output_bias_total = totals[2 * model_width : 3 * model_width]
    bias_total = totals[3 * model_width :]
    heads_bias_total = bias_total[: 3 * width].reshape(3, width)
    expand_bias_total = bias_total[3 * width :]

    scale_back = 1.0 / seq_len
    norm_upd, norm_mom = adam_update(norm_moments, norm_total * scale_back)
    hbias_upd, hbias_mom = adam_update(heads_bias_moments, heads_bias_total * scale_back)
    ebias_upd, ebias_mom = adam_update(expand_bias_moments, expand_bias_total * scale_back)
    output_bias_grad = jnp.stack([output_bias_total, output_bias_total]) * scale_back
    obias_upd, obias_mom = adam_update(output_bias_moments, output_bias_grad)
    return (
        output,
        input_grad,
        norm_upd,
        norm_mom,
        heads_upd,
        heads_mom,
        hbias_upd,
        hbias_mom,
        merge_upd,
        merge_mom,
        expand_upd,
        expand_mom,
        ebias_upd,
        ebias_mom,
        shrink_upd,
        shrink_mom,
        obias_upd,
        obias_mom,
    )


def solution(mesh):
    placed = (
        P("dp", "tensor", None),
        P("dp", "tensor", None),
        P("dp", None),
        P("dp", None),
        P(),
        P(),
        P(None, "dp", "tensor"),
        P(None, None, "dp", "tensor"),
        P(None, "tensor"),
        P(None, None, "tensor"),
        P("tensor", "dp"),
        P(None, "tensor", "dp"),
        P("dp", "tensor"),
        P(None, "dp", "tensor"),
        P("tensor"),
        P(None, "tensor"),
        P("tensor", "dp"),
        P(None, "tensor", "dp"),
        P(),
        P(),
    )
    return jax.shard_map(
        body,
        mesh=mesh,
        in_specs=placed,
        out_specs=(placed[0], placed[0], P(), P(), *placed[6:18], P(), P()),
        check_vma=False,
    )
```

profile of v0, /device:TPU:0, one launch (start us, length us, event | category | flops | bytes accessed | tf_op | source)
XLA Modules:
  0.0 402.0 jit_solution(8820261616347509391)
XLA Ops:
  7.3 1.7 constant_dynamic-slice_fusion.3
  14.9 3.0 collective-permute-start
  21.6 1.9 convert.22
  26.5 31.5 %collective-permute-done.refs_9_.refs_10_.refs_11_.refs_4_.refs_5_ = bf16[512,1792]{1,0:T(8,128)(2,1)} collective-permute-done((bf16[512,1792]{1,0:T(8,128)(2,1)S(1)}, bf16[512,1792]{1,0:T(8,128)(2,1)}, u32[]{:S(2)}, u32[]{:S(2)}) %collective-permute-start) | collective-permute-done | bytes 1835040 | tf_op jit(solution)/shard_map/ppermute | solution.py:702
  59.2 1.8 collective-permute-start.2
  63.9 7.2 %select_convert_fusion = (bf16[2,1024,1024]{2,1,0:T(8,128)(2,1)}, bf16[2,1024,1024]{2,1,0:T(8,128)(2,1)}) fusion(s32[2,1024]{1,0:T(2,128)S(1)} %get-tuple-element.155, pred[1024,1024]{1,0:T(8,128)(4,1)S(1)} %get-tuple-element.163, pred[2,1024]{1,0:T(4,128)(4,1)S(1)} %broadcast_compare_fusion, pred[1024,1024]{1,0:T(8,128)(4,1)S(1)} %get-tuple-element.164, ...), kind=kLoop, calls=%fused_computation | loop fusion | flops 25165824 | bytes 12593152 | tf_op jit(solution)/shard_map/vmap()/convert_element_type | solution.py:52
  71.1 9.8 %collective-permute-done.2.refs_15_.refs_16_.refs_17_.refs_6_.refs_1_.refs_7_ = bf16[256,1792]{1,0:T(8,128)(2,1)S(1)} collective-permute-done((bf16[256,1792]{1,0:T(8,128)(2,1)S(1)}, bf16[256,1792]{1,0:T(8,128)(2,1)S(1)}, u32[]{:S(2)}, u32[]{:S(2)}) %collective-permute-start.2) | collective-permute-done | bytes 917536 | tf_op jit(solution)/shard_map/ppermute | solution.py:702
  80.8 2.5 collective-permute-done.3.refs_18_.refs_19_.refs_20_.refs_7_.refs_2_.refs_8_
  86.3 5.5 %fusion.10 = (f32[2,1024,128]{2,1,0:T(8,128)}, f32[2,1024,128]{2,1,0:T(8,128)}) fusion(f32[128]{0:T(128)S(1)} %compare_select_fusion, f32[128]{0:T(128)S(1)} %mul.306, f32[2,1024]{1,0:T(2,128)S(1)} %get-tuple-element.154), kind=kLoop, calls=%fused_computation.28 | loop fusion | flops 524288 | bytes 2106368 | tf_op jit(solution)/shard_map/vmap()/mul | solution.py:44
  91.8 4.4 %all-gather.3.cloned.1.call-done.refs_1_ = bf16[2,1024,2048]{2,1,0:T(8,128)(2,1)} async-done(((bf16[2,128,2048]{2,1,0:T(8,128)(2,1)}), bf16[2,1024,2048]{2,1,0:T(8,128)(2,1)}) %all-gather.3.cloned.1.call-update) | async-done | bytes 8388624 | tf_op jit(solution)/shard_map/all_gather | solution.py:847
  96.1 23.1 %attend.1 = (bf16[3,2,1024,256]{3,2,1,0:T(8,128)(2,1)}, bf16[2,1024,256]{2,1,0:T(8,128)(2,1)}, f32[2,8,1024]{2,1,0:T(8,128)}) custom-call(s32[2,4]{1,0:T(2,128)} %and_select_fusion.1.first_ref, bf16[2,1024,1024]{2,1,0:T(8,128)(2,1)} %get-tuple-element.149.refs_0_.refs_7_, bf16[2,1024,2048]{2,1,0:T(8,128)(2,1)} %all-gather.3.cloned.1.call-done.refs_1_, ...), custom_call_target="tpu_custom_call" | custom-call | flops 10000000000 | bytes 10000000 | tf_op jit(solution)/shard_map/attend/pallas_call | solution.py:101
  121.9 2.3 collective-permute-start.6
  125.3 1.8 collective-permute-start.7
  127.1 17.7 %gelu_units.1 = (bf16[2,1024,1024]{2,1,0:T(8,128)(2,1)}, bf16[2,1024,1024]{2,1,0:T(8,128)(2,1)}) custom-call(s32[1]{0:T(128)} %bitcast.1.first_ref, bf16[3,2,1024,256]{3,2,1,0:T(8,128)(2,1)} %get-tuple-element.59.refs_0_.refs_1_.refs_2_.refs_3_, bf16[2,1024,2048]{2,1,0:T(8,128)(2,1)} %all-gather.3.cloned.1.call-done.refs_1_, f32[1,1024]{1,0:T(1,128)} %bitcast.103, ...), custom_call_target="tpu_custom_call" | custom-call | flops 10000000000 | bytes 10000000 | tf_op jit(solution)/shard_map/gelu_units/pallas_call | solution.py:101
  145.9 17.0 %out_sums.1.refs_0_ = bf16[2,1024,2048]{2,1,0:T(8,128)(2,1)} custom-call(s32[1]{0:T(128)} %bitcast.1.first_ref, bf16[2,1024,1024]{2,1,0:T(8,128)(2,1)} %get-tuple-element.60.refs_0_.refs_2_, bf16[2,1024,256]{2,1,0:T(8,128)(2,1)} %get-tuple-element.61.refs_2_.refs_1_.refs_4_, bf16[2,1024,1024]{2,1,0:T(8,128)(2,1)} %get-tuple-element.60.refs_0_.refs_2_, ...), custom_call_target="tpu_custom_call" | custom-call | flops 10000000000 | bytes 10000000 | tf_op jit(solution)/shard_map/out_sums/pallas_call | solution.py:101
  162.9 15.4 %all-gather.5.cloned.1.call-done.refs_5_.refs_1_ = bf16[2,1024,2048]{2,1,0:T(8,128)(2,1)} async-done(((bf16[2,128,2048]{2,1,0:T(8,128)(2,1)}), bf16[2,1024,2048]{2,1,0:T(8,128)(2,1)}) %all-gather.5.cloned.1.call-update) | async-done | bytes 8388624 | tf_op jit(solution)/shard_map/all_gather | solution.py:847
  178.3 19.9 %exit_grad.1 = (bf16[1280,256]{1,0:T(8,128)(2,1)}, bf16[1280,256]{1,0:T(8,128)(2,1)}, bf16[1280,512]{1,0:T(8,128)(2,1)}, bf16[1280,512]{1,0:T(8,128)(2,1)}, bf16[1280,512]{1,0:T(8,128)(2,1)}) custom-call(s32[1]{0:T(128)} %bitcast.1.first_ref, bf16[2,1024,2048]{2,1,0:T(8,128)(2,1)} %out_sums.1.refs_0_, bf16[2048,1024]{1,0:T(8,128)(2,1)} %bitcast.105, ...), custom_call_target="tpu_custom_call" | custom-call | flops 10000000000 | bytes 10000000 | tf_op jit(solution)/shard_map/exit_grad/pallas_call | solution.py:101
  203.5 30.8 %attend_back.1 = (bf16[2,1024,768]{2,1,0:T(8,128)(2,1)}, f32[8,256]{1,0:T(8,128)}) custom-call(s32[2,4]{1,0:T(2,128)} %and_select_fusion.1.first_ref, bf16[1280,256]{1,0:T(8,128)(2,1)} %get-tuple-element.64.refs_0_, bf16[3,2,1024,256]{3,2,1,0:T(8,128)(2,1)} %get-tuple-element.59.refs_0_.refs_1_.refs_2_.refs_3_, ...), custom_call_target="tpu_custom_call" | custom-call | flops 10000000000 | bytes 10000000 | tf_op jit(solution)/shard_map/attend_back/pallas_call | solution.py:101
  241.7 32.8 %back_rows.1 = (bf16[2,1024,1024]{2,1,0:T(8,128)(2,1)}, bf16[2,1024,2048]{2,1,0:T(8,128)(2,1)}, f32[8,1024]{1,0:T(8,128)}) custom-call(s32[1]{0:T(128)} %bitcast.1.first_ref, bf16[2,1024,768]{2,1,0:T(8,128)(2,1)} %get-tuple-element.66.refs_0_.refs_3_.refs_2_, bf16[2,1024,2048]{2,1,0:T(8,128)(2,1)} %all-gather.5.cloned.1.call-done.refs_5_.refs_1_, ...), custom_call_target="tpu_custom_call" | custom-call | flops 10000000000 | bytes 10000000 | tf_op jit(solution)/shard_map/back_rows/pallas_call | solution.py:101
  276.1 15.7 %expand_grad.1 = (bf16[256,1024]{1,0:T(8,128)(2,1)}, bf16[256,1024]{1,0:T(8,128)(2,1)}, bf16[512,1024]{1,0:T(8,128)(2,1)}, bf16[512,1024]{1,0:T(8,128)(2,1)}, bf16[512,1024]{1,0:T(8,128)(2,1)}) custom-call(s32[1]{0:T(128)} %bitcast.1.first_ref, bf16[2,1024,1024]{2,1,0:T(8,128)(2,1)} %get-tuple-element.68.refs_0_, ...), custom_call_target="tpu_custom_call" | custom-call | flops 10000000000 | bytes 10000000 | tf_op jit(solution)/shard_map/expand_grad/pallas_call | solution.py:101
  293.7 14.0 %heads_grad.1 = (bf16[256,768]{1,0:T(8,128)(2,1)}, bf16[256,768]{1,0:T(8,128)(2,1)}, bf16[512,768]{1,0:T(8,128)(2,1)}, bf16[512,768]{1,0:T(8,128)(2,1)}, bf16[512,768]{1,0:T(8,128)(2,1)}) custom-call(s32[1]{0:T(128)} %bitcast.1.first_ref, bf16[256,1024]{1,0:T(8,128)(2,1)} %get-tuple-element.69.refs_0_, bf16[2048,2048]{1,0:T(8,128)(2,1)} %bitcast.87, ...), custom_call_target="tpu_custom_call" | custom-call | flops 10000000000 | bytes 10000000 | tf_op jit(solution)/shard_map/heads_grad/pallas_call | solution.py:101
  307.7 1.9 copy.75.refs_0_
  319.6 7.6 %adam_sum.4 = (f32[1024,512]{1,0:T(8,128)}, f32[2,1024,512]{2,1,0:T(8,128)}) custom-call(s32[1]{0:T(128)} %bitcast.1.first_ref, bf16[256,768]{1,0:T(8,128)(2,1)} %get-tuple-element.70.refs_0_, bf16[256,768]{1,0:T(8,128)(2,1)} %get-tuple-element.73.refs_1_, bf16[256,768]{1,0:T(8,128)(2,1)} %get-tuple-element.74.refs_2_, f32[2,1024,512]{2,1,0:T(8,128)} %refs_3_.3, ...), custom_call_target="tpu_custom_call" | custom-call | flops 10000000000 | bytes 10000000 | tf_op jit(solution)/shard_map/adam_sum/pallas_call | solution.py:101
  327.2 3.7 adam_sum.5
  334.5 2.6 layer_output.1.refs_0_
  337.1 11.0 %collective-permute-done.17.refs_4_ = bf16[512,1024]{1,0:T(8,128)(2,1)} collective-permute-done((bf16[512,1024]{1,0:T(8,128)(2,1)S(1)}, bf16[512,1024]{1,0:T(8,128)(2,1)}, u32[]{:S(2)}, u32[]{:S(2)}) %collective-permute-start.17) | collective-permute-done | bytes 1048608 | tf_op jit(solution)/shard_map/ppermute | solution.py:702
  348.1 6.6 %adam_sum.6 = (f32[512,1024]{1,0:T(8,128)}, f32[2,512,1024]{2,1,0:T(8,128)}) custom-call(s32[1]{0:T(128)} %bitcast.1.first_ref, bf16[2,128,2048]{2,1,0:T(8,128)(2,1)} %layer_output.1.refs_0_, f32[2,512,1024]{2,1,0:T(8,128)} %refs_1_.4, bf16[512,1024]{1,0:T(8,128)(2,1)} %get-tuple-element.83.refs_2_, bf16[512,1024]{1,0:T(8,128)(2,1)} %collective-permute-done.16.refs_3_, ...), custom_call_target="tpu_custom_call" | custom-call | flops 10000000000 | bytes 10000000 | tf_op jit(solution)/shard_map/adam_sum/pallas_call | solution.py:101
  354.7 7.4 %collective-permute-done.19.refs_2_.refs_4_ = bf16[512,768]{1,0:T(8,128)(2,1)} collective-permute-done((bf16[512,768]{1,0:T(8,128)(2,1)S(1)}, bf16[512,768]{1,0:T(8,128)(2,1)}, u32[]{:S(2)}, u32[]{:S(2)}) %collective-permute-start.19) | collective-permute-done | bytes 786464 | tf_op jit(solution)/shard_map/ppermute | solution.py:702
  363.2 4.8 %input_grad.1 = (bf16[2,128,2048]{2,1,0:T(8,128)(2,1)}, f32[8,2048]{1,0:T(8,128)}) custom-call(s32[1]{0:T(128)} %bitcast.first_ref, f32[512,1024]{1,0:T(8,128)} %get-tuple-element.110.refs_0_, bf16[512,768]{1,0:T(8,128)(2,1)} %copy-done.30, bf16[512,768]{1,0:T(8,128)(2,1)} %collective-permute-done.19.refs_2_.refs_4_, bf16[2,128,2048]{2,1,0:T(8,128)(2,1)} %refs_3_.5, ...), custom_call_target="tpu_custom_call" | custom-call | flops 10000000000 | bytes 10000000 | tf_op jit(solution)/shard_map/input_grad/pallas_call | solution.py:101
  371.9 2.9 collective-permute-start.23
  375.6 3.4 collective-permute-done.22
  382.6 7.3 %adam_sum.7 = (f32[3,512,256]{2,1,0:T(8,128)}, f32[2,3,512,256]{3,2,1,0:T(8,128)}) custom-call(s32[1]{0:T(128)} %bitcast.1.first_ref, bf16[2,128,2048]{2,1,0:T(8,128)(2,1)} %get-tuple-element.101.refs_0_, f32[2,3,512,256]{3,2,1,0:T(8,128)} %refs_1_.5, bf16[512,768]{1,0:T(8,128)(2,1)} %get-tuple-element.94.refs_2_, bf16[512,768]{1,0:T(8,128)(2,1)} %copy-done.30, ...), custom_call_target="tpu_custom_call" | custom-call | flops 10000000000 | bytes 10000000 | tf_op jit(solution)/shard_map/adam_sum/pallas_call | solution.py:101
  (216 shorter events, 68.4 us)
Async XLA Ops:
  7.2 88.9 %all-gather.3.cloned.1.call-start = ((), (), s32[]{:S(2)}) async-start(), calls=%async_computation.2 | async-start | bytes 9437184 | tf_op jit(solution)/shard_map/all_gather | solution.py:847
  11.2 167.1 %all-gather.5.cloned.1.call-start = ((), (), s32[]{:S(2)}) async-start(), calls=%async_computation.3 | async-start | bytes 9437184 | tf_op jit(solution)/shard_map/all_gather | solution.py:847
  12.4 263.7 %reduce-scatter.3.cloned.1.call-start = ((), (), s32[]{:S(2)}) async-start(), calls=%async_computation.4 | async-start | bytes 9437184 | tf_op jit(solution)/shard_map/reduce_scatter | solution.py:850
  14.9 43.1 %collective-permute-start = (bf16[512,1792]{1,0:T(8,128)(2,1)S(1)}, bf16[512,1792]{1,0:T(8,128)(2,1)}, u32[]{:S(2)}, u32[]{:S(2)}) collective-permute-start(bf16[512,1792]{1,0:T(8,128)(2,1)S(1)} %pad_maximum_fusion.refs_6_.refs_7_.refs_8_.refs_3_.refs_4_), channel_id=1, source_target_pairs={{0,8},{8,0},{16,24},{24,16},{1,9},{9,1},{17,25},{25,17},{2,10},{10... | collective-permute-start | bytes 5505032 | tf_op jit(solution)/shard_map/ppermute | solution.py:702
  17.9 43.2 %collective-permute-start.1 = (bf16[512,1792]{1,0:T(8,128)(2,1)S(1)}, bf16[512,1792]{1,0:T(8,128)(2,1)}, u32[]{:S(2)}, u32[]{:S(2)}) collective-permute-start(bf16[512,1792]{1,0:T(8,128)(2,1)S(1)} %pad_maximum_fusion.refs_6_.refs_7_.refs_8_.refs_3_.refs_4_), channel_id=1, source_target_pairs={{0,16},{8,24},{16,0},{24,8},{1,17},{9,25},{17,1},{25,9},{2,18},{10... | collective-permute-start | bytes 5505032 | tf_op jit(solution)/shard_map/ppermute | solution.py:702
  59.2 21.6 %collective-permute-start.2 = (bf16[256,1792]{1,0:T(8,128)(2,1)S(1)}, bf16[256,1792]{1,0:T(8,128)(2,1)S(1)}, u32[]{:S(2)}, u32[]{:S(2)}) collective-permute-start(bf16[256,1792]{1,0:T(8,128)(2,1)S(1)} %slice.217), channel_id=1, source_target_pairs={{0,16},{8,24},{16,0},{24,8},{1,17},{9,25},{17,1},{25,9},{2,18},{10... | collective-permute-start | bytes 2752520 | tf_op jit(solution)/shard_map/ppermute | solution.py:702
  62.3 21.0 %collective-permute-start.3 = (bf16[256,1792]{1,0:T(8,128)(2,1)S(1)}, bf16[256,1792]{1,0:T(8,128)(2,1)S(1)}, u32[]{:S(2)}, u32[]{:S(2)}) collective-permute-start(bf16[256,1792]{1,0:T(8,128)(2,1)S(1)} %slice.218), channel_id=1, source_target_pairs={{0,8},{8,0},{16,24},{24,16},{1,9},{9,1},{17,25},{25,17},{2,10},{10... | collective-permute-start | bytes 2752520 | tf_op jit(solution)/shard_map/ppermute | solution.py:702
  84.3 35.0 %collective-permute-start.4 = (bf16[1280,512]{1,0:T(8,128)(2,1)}, bf16[1280,512]{1,0:T(8,128)(2,1)S(1)}, u32[]{:S(2)}, u32[]{:S(2)}) collective-permute-start(bf16[1280,512]{1,0:T(8,128)(2,1)} %hold.5.refs_3_.refs_10_.refs_9_), channel_id=1, source_target_pairs={{0,8},{8,0},{16,24},{24,16},{1,9},{9,1},{17,25},{25,17},{2,10},{10... | collective-permute-start | bytes 3932168 | tf_op jit(solution)/shard_map/ppermute | solution.py:702
  85.7 33.5 %collective-permute-start.5 = (bf16[1280,512]{1,0:T(8,128)(2,1)}, bf16[1280,512]{1,0:T(8,128)(2,1)S(1)}, u32[]{:S(2)}, u32[]{:S(2)}) collective-permute-start(bf16[1280,512]{1,0:T(8,128)(2,1)} %hold.5.refs_3_.refs_10_.refs_9_), channel_id=1, source_target_pairs={{0,16},{8,24},{16,0},{24,8},{1,17},{9,25},{17,1},{25,9},{2,18},{10... | collective-permute-start | bytes 3932168 | tf_op jit(solution)/shard_map/ppermute | solution.py:702
  121.9 22.9 %collective-permute-start.6 = (bf16[1280,256]{1,0:T(8,128)(2,1)S(1)}, bf16[1280,256]{1,0:T(8,128)(2,1)S(1)}, u32[]{:S(2)}, u32[]{:S(2)}) collective-permute-start(bf16[1280,256]{1,0:T(8,128)(2,1)S(1)} %slice.181), channel_id=1, source_target_pairs={{0,16},{8,24},{16,0},{24,8},{1,17},{9,25},{17,1},{25,9},{2,18},{10... | collective-permute-start | bytes 1966088 | tf_op jit(solution)/shard_map/ppermute | solution.py:702
  125.3 19.5 %collective-permute-start.7 = (bf16[1280,256]{1,0:T(8,128)(2,1)S(1)}, bf16[1280,256]{1,0:T(8,128)(2,1)S(1)}, u32[]{:S(2)}, u32[]{:S(2)}) collective-permute-start(bf16[1280,256]{1,0:T(8,128)(2,1)S(1)} %slice.182), channel_id=1, source_target_pairs={{0,8},{8,0},{16,24},{24,16},{1,9},{9,1},{17,25},{25,17},{2,10},{10... | collective-permute-start | bytes 1966088 | tf_op jit(solution)/shard_map/ppermute | solution.py:702
  162.9 200.3 %reduce-scatter.5.cloned.1.call-start = ((), (), s32[]{:S(2)}) async-start(), calls=%async_computation.5 | async-start | bytes 9437184 | tf_op jit(solution)/shard_map/reduce_scatter | solution.py:850
  198.2 36.0 %collective-permute-start.10 = (bf16[1280,256]{1,0:T(8,128)(2,1)}, bf16[1280,256]{1,0:T(8,128)(2,1)S(1)}, u32[]{:S(2)}, u32[]{:S(2)}) collective-permute-start(bf16[1280,256]{1,0:T(8,128)(2,1)} %get-tuple-element.64.refs_0_), channel_id=1, source_target_pairs={{0,8},{8,0},{16,24},{24,16},{1,9},{9,1},{17,25},{25,17},{2,10},{10... | collective-permute-start | bytes 1966088 | tf_op jit(solution)/shard_map/ppermute | solution.py:702
  199.7 34.6 %collective-permute-start.11 = (bf16[1280,256]{1,0:T(8,128)(2,1)}, bf16[1280,256]{1,0:T(8,128)(2,1)S(1)}, u32[]{:S(2)}, u32[]{:S(2)}) collective-permute-start(bf16[1280,256]{1,0:T(8,128)(2,1)} %get-tuple-element.77), channel_id=1, source_target_pairs={{0,16},{8,24},{16,0},{24,8},{1,17},{9,25},{17,1},{25,9},{2,18},{10... | collective-permute-start | bytes 1966088 | tf_op jit(solution)/shard_map/ppermute | solution.py:702
  238.1 36.5 %collective-permute-start.13 = (bf16[1280,512]{1,0:T(8,128)(2,1)}, bf16[1280,512]{1,0:T(8,128)(2,1)S(1)}, u32[]{:S(2)}, u32[]{:S(2)}) collective-permute-start(bf16[1280,512]{1,0:T(8,128)(2,1)} %pad_maximum_fusion.3), channel_id=1, source_target_pairs={{0,16},{8,24},{16,0},{24,8},{1,17},{9,25},{17,1},{25,9},{2,18},{10... | collective-permute-start | bytes 3932168 | tf_op jit(solution)/shard_map/ppermute | solution.py:702
  240.6 34.0 %collective-permute-start.12 = (bf16[1280,512]{1,0:T(8,128)(2,1)}, bf16[1280,512]{1,0:T(8,128)(2,1)S(1)}, u32[]{:S(2)}, u32[]{:S(2)}) collective-permute-start(bf16[1280,512]{1,0:T(8,128)(2,1)} %pad_maximum_fusion.2), channel_id=1, source_target_pairs={{0,8},{8,0},{16,24},{24,16},{1,9},{9,1},{17,25},{25,17},{2,10},{10... | collective-permute-start | bytes 3932168 | tf_op jit(solution)/shard_map/ppermute | solution.py:702
  291.9 19.9 %collective-permute-start.8 = (bf16[256,1024]{1,0:T(8,128)(2,1)}, bf16[256,1024]{1,0:T(8,128)(2,1)S(1)}, u32[]{:S(2)}, u32[]{:S(2)}) collective-permute-start(bf16[256,1024]{1,0:T(8,128)(2,1)} %get-tuple-element.69.refs_0_), channel_id=1, source_target_pairs={{0,8},{8,0},{16,24},{24,16},{1,9},{9,1},{17,25},{25,17},{2,10},{10... | collective-permute-start | bytes 1572872 | tf_op jit(solution)/shard_map/ppermute | solution.py:702
  292.7 19.0 %collective-permute-start.9 = (bf16[256,1024]{1,0:T(8,128)(2,1)}, bf16[256,1024]{1,0:T(8,128)(2,1)S(1)}, u32[]{:S(2)}, u32[]{:S(2)}) collective-permute-start(bf16[256,1024]{1,0:T(8,128)(2,1)} %get-tuple-element.72), channel_id=1, source_target_pairs={{0,16},{8,24},{16,0},{24,8},{1,17},{9,25},{17,1},{25,9},{2,18},{10... | collective-permute-start | bytes 1572872 | tf_op jit(solution)/shard_map/ppermute | solution.py:702
  312.7 18.1 %collective-permute-start.14 = (bf16[256,768]{1,0:T(8,128)(2,1)}, bf16[256,768]{1,0:T(8,128)(2,1)S(1)}, u32[]{:S(2)}, u32[]{:S(2)}) collective-permute-start(bf16[256,768]{1,0:T(8,128)(2,1)} %get-tuple-element.73.refs_1_), channel_id=1, source_target_pairs={{0,8},{8,0},{16,24},{24,16},{1,9},{9,1},{17,25},{25,17},{2,10},{10... | collective-permute-start | bytes 1179656 | tf_op jit(solution)/shard_map/ppermute | solution.py:702
  313.3 18.9 %collective-permute-start.15 = (bf16[256,768]{1,0:T(8,128)(2,1)}, bf16[256,768]{1,0:T(8,128)(2,1)}, u32[]{:S(2)}, u32[]{:S(2)}) collective-permute-start(bf16[256,768]{1,0:T(8,128)(2,1)} %get-tuple-element.74.refs_2_), channel_id=1, source_target_pairs={{0,16},{8,24},{16,0},{24,8},{1,17},{9,25},{17,1},{25,9},{2,18},{10... | collective-permute-start | bytes 1179656 | tf_op jit(solution)/shard_map/ppermute | solution.py:702
  316.4 31.7 %collective-permute-start.17 = (bf16[512,1024]{1,0:T(8,128)(2,1)S(1)}, bf16[512,1024]{1,0:T(8,128)(2,1)}, u32[]{:S(2)}, u32[]{:S(2)}) collective-permute-start(bf16[512,1024]{1,0:T(8,128)(2,1)S(1)} %pad_maximum_fusion.7), channel_id=1, source_target_pairs={{0,16},{8,24},{16,0},{24,8},{1,17},{9,25},{17,1},{25,9},{2,18},{10... | collective-permute-start | bytes 3145736 | tf_op jit(solution)/shard_map/ppermute | solution.py:702
  318.1 30.0 %collective-permute-start.16 = (bf16[512,1024]{1,0:T(8,128)(2,1)}, bf16[512,1024]{1,0:T(8,128)(2,1)}, u32[]{:S(2)}, u32[]{:S(2)}) collective-permute-start(bf16[512,1024]{1,0:T(8,128)(2,1)} %pad_maximum_fusion.6), channel_id=1, source_target_pairs={{0,8},{8,0},{16,24},{24,16},{1,9},{9,1},{17,25},{25,17},{2,10},{10... | collective-permute-start | bytes 3145736 | tf_op jit(solution)/shard_map/ppermute | solution.py:702
  331.1 31.0 %collective-permute-start.19 = (bf16[512,768]{1,0:T(8,128)(2,1)S(1)}, bf16[512,768]{1,0:T(8,128)(2,1)}, u32[]{:S(2)}, u32[]{:S(2)}) collective-permute-start(bf16[512,768]{1,0:T(8,128)(2,1)S(1)} %pad_maximum_fusion.9), channel_id=1, source_target_pairs={{0,16},{8,24},{16,0},{24,8},{1,17},{9,25},{17,1},{25,9},{2,18},{10... | collective-permute-start | bytes 2359304 | tf_op jit(solution)/shard_map/ppermute | solution.py:702
  333.4 28.7 %collective-permute-start.18 = (bf16[512,768]{1,0:T(8,128)(2,1)S(1)}, bf16[512,768]{1,0:T(8,128)(2,1)S(1)}, u32[]{:S(2)}, u32[]{:S(2)}) collective-permute-start(bf16[512,768]{1,0:T(8,128)(2,1)S(1)} %pad_maximum_fusion.8), channel_id=1, source_target_pairs={{0,8},{8,0},{16,24},{24,16},{1,9},{9,1},{17,25},{25,17},{2,10},{10... | collective-permute-start | bytes 2359304 | tf_op jit(solution)/shard_map/ppermute | solution.py:702
  363.2 12.4 %copy-start.29 = (f32[8,256]{1,0:T(8,128)S(1)}, f32[8,256]{1,0:T(8,128)}, u32[]{:S(2)}) copy-start(f32[8,256]{1,0:T(8,128)} %get-tuple-element.92) | copy-start | bytes 24580
  368.0 1.5 collective-permute-start.20
  370.4 5.3 %collective-permute-start.21 = (f32[8,2048]{1,0:T(8,128)S(1)}, f32[8,2048]{1,0:T(8,128)S(1)}, u32[]{:S(2)}, u32[]{:S(2)}) collective-permute-start(f32[8,2048]{1,0:T(8,128)S(1)} %add.167), channel_id=1, source_target_pairs={{0,2},{1,3},{2,0},{3,1},{4,6},{5,7},{6,4},{7,5},{8,10},{9,11},{10,... | collective-permute-start | bytes 196616 | tf_op jit(solution)/shard_map/ppermute | solution.py:782
  370.4 8.6 %collective-permute-start.22 = (f32[8,2048]{1,0:T(8,128)S(1)}, f32[8,2048]{1,0:T(8,128)S(1)}, u32[]{:S(2)}, u32[]{:S(2)}) collective-permute-start(f32[8,2048]{1,0:T(8,128)S(1)} %add.167), channel_id=1, source_target_pairs={{0,4},{1,5},{2,6},{3,7},{4,0},{5,1},{6,2},{7,3},{8,12},{9,13},{10,... | collective-permute-start | bytes 196616 | tf_op jit(solution)/shard_map/ppermute | solution.py:782
  371.9 7.1 %collective-permute-start.23 = (f32[8,2048]{1,0:T(8,128)S(1)}, f32[8,2048]{1,0:T(8,128)S(1)}, u32[]{:S(2)}, u32[]{:S(2)}) collective-permute-start(f32[8,2048]{1,0:T(8,128)S(1)} %add.167), channel_id=1, source_target_pairs={{0,6},{1,7},{2,4},{3,5},{4,2},{5,3},{6,0},{7,1},{8,14},{9,15},{10,... | collective-permute-start | bytes 196616 | tf_op jit(solution)/shard_map/ppermute | solution.py:782
  379.1 10.8 %collective-permute-start.24 = (f32[7936]{0:T(1024)S(1)}, f32[7936]{0:T(1024)S(1)}, u32[]{:S(2)}, u32[]{:S(2)}) collective-permute-start(f32[7936]{0:T(1024)S(1)} %pad_maximum_fusion.10), channel_id=1, source_target_pairs={{0,8},{8,0},{16,24},{24,16},{1,9},{9,1},{17,25},{25,17},{2,10},{10... | collective-permute-start | bytes 95240 | tf_op jit(solution)/shard_map/ppermute | solution.py:782
  380.8 9.2 %collective-permute-start.25 = (f32[7936]{0:T(1024)S(1)}, f32[7936]{0:T(1024)S(1)}, u32[]{:S(2)}, u32[]{:S(2)}) collective-permute-start(f32[7936]{0:T(1024)S(1)} %pad_maximum_fusion.10), channel_id=1, source_target_pairs={{0,16},{8,24},{16,0},{24,8},{1,17},{9,25},{17,1},{25,9},{2,18},{10... | collective-permute-start | bytes 95240 | tf_op jit(solution)/shard_map/ppermute | solution.py:782
  382.2 7.7 %collective-permute-start.26 = (f32[7936]{0:T(1024)S(1)}, f32[7936]{0:T(1024)S(1)}, u32[]{:S(2)}, u32[]{:S(2)}) collective-permute-start(f32[7936]{0:T(1024)S(1)} %pad_maximum_fusion.10), channel_id=1, source_target_pairs={{0,24},{8,16},{16,8},{24,0},{1,25},{9,17},{17,9},{25,1},{2,26},{10... | collective-permute-start | bytes 95240 | tf_op jit(solution)/shard_map/ppermute | solution.py:782
  (32 other events, 118.9 us)
Sparse Core Ops, SparseCore 0:
  11.3 84.7 all-gather.2
  97.7 80.5 all-gather.4
  180.6 88.1 reduce-scatter.2
  276.2 86.9 reduce-scatter.4
where the time goes:
time: 408 us; the launch traced here: 402 us
  Pallas kernels  204 us (50%)
  waiting for transfers between devices  88 us (22%)
  other arithmetic  37.3 us (9%)
  starting transfers between devices  35.5 us (9%)
  local copies, waits for them, and re-layouts  22.9 us (6%)
  between operations  14.7 us (4%)
    pallas_call x14, Pallas kernels, staged(): pl.pallas_call(without, grid_spec=pltpu.PrefetchScalarGridSpec(num_scalar...  204 us
    ppermute x20, waiting for transfers between devices, swap(): return lax.ppermute(array, 'dp', [(i, i ^ distance) for i in range(size)])  62.1 us
    ppermute x20, starting transfers between devices, swap(): return lax.ppermute(array, 'dp', [(i, i ^ distance) for i in range(size)])  27.4 us
    all_gather x2, waiting for transfers between devices, gather_rows(): return lax.all_gather(array, 'tensor', axis=1, tiled=True)  19.8 us
    unnamed x68, local copies, waits for them, and re-layouts  9.98 us
  transfers between devices with their start and end apart: 31, of which 11 were waited for; matrix products, arithmetic and copies ran while one was open for 11% of the time, Pallas kernels for 49%

commit v1 on v0

--- a/solution.py
+++ b/solution.py
@@ -94,7 +94,9 @@
     return pl.BlockSpec(shape, lambda *_: place, pipeline_mode=one)
 
 
-def staged(kernel, after, first, inputs, out_shape, name, grid, in_specs, out_specs, scratch_shapes=()):
+def staged(
+    kernel, after, first, inputs, out_shape, name, grid, in_specs, out_specs, scratch_shapes=(), flops=10**10
+):
     def without(first_ref, *refs):
         kernel(first_ref, *refs[len(after) :])
 
@@ -109,7 +111,7 @@
         ),
         out_shape=out_shape,
         compiler_params=pltpu.CompilerParams(vmem_limit_bytes=VMEM * 1024 * 1024),
-        cost_estimate=pl.CostEstimate(flops=10**10, bytes_accessed=10**7, transcendentals=0),
+        cost_estimate=pl.CostEstimate(flops=flops, bytes_accessed=flops // 1000, transcendentals=0),
         name=name,
     )(first, *after, *inputs)
 
@@ -131,7 +133,7 @@
 
 
 def attend_kernel(lows, first, low_ref, x_ref, bias_ref, cos_ref, sin_ref, mask_ref, *refs):
-    *weights, qkv_ref, out_ref, lse_ref, k_all, v_all = refs
+    *weights, qkv_ref, out_ref, rest_ref, lse_ref, k_all, v_all = refs
     seq, step = pl.program_id(0), pl.program_id(1)
     rows, width = out_ref.shape
     heads = width // HEAD_DIM
@@ -177,7 +179,9 @@
                 mixed = nn(weights.astype(bf16), values) * (1.0 / total)
                 result = jnp.where(mine, mixed, result)
                 stats = jnp.where(lane == head, top + jnp.log(total), stats)
-            out_ref[...] = result.astype(bf16)
+            low_result = result.astype(bf16)
+            out_ref[...] = low_result
+            rest_ref[...] = (result - low_result.astype(f32)).astype(bf16)
             lse_ref[...] = jnp.transpose(stats)[: lse_ref.shape[0], :]
 
 
@@ -199,6 +203,7 @@
         [normed, bias, cosine, sine, mask, *[piece for piece in pieces for _ in range(3)]],
         [
             jax.ShapeDtypeStruct((3, count, seq_len, width), bf16),
+            jax.ShapeDtypeStruct((count, seq_len, width), bf16),
             jax.ShapeDtypeStruct((count, seq_len, width), bf16),
             jax.ShapeDtypeStruct((count, stat_rows, seq_len), f32),
         ],
@@ -219,6 +224,7 @@
         out_specs=[
             pl.BlockSpec((3, None, rows, width), lambda s, i, low: (0, s, i, 0)),
             pl.BlockSpec((None, rows, width), lambda s, i, low: (s, i, 0)),
+            pl.BlockSpec((None, rows, width), lambda s, i, low: (s, i, 0)),
             pl.BlockSpec((None, stat_rows, rows), lambda s, i, low: (s, 0, i)),
         ],
         scratch_shapes=[pltpu.VMEM((seq_len, width), bf16), pltpu.VMEM((seq_len, width), bf16)],
@@ -226,7 +232,7 @@
 
 
 def attend_back_kernel(
-    lows, first, low_ref, q_ref, k_ref, v_ref, o_ref, g_ref, lse_ref, mask_ref, cos_ref, sin_ref, *refs
+    lows, first, low_ref, q_ref, k_ref, v_ref, o_ref, rest_ref, g_ref, lse_ref, mask_ref, cos_ref, sin_ref, *refs
 ):
     *weights, out_ref, sum_ref, dk_all, dv_all, k_turned = refs
     seq, step = pl.program_id(0), pl.program_id(1)
@@ -253,7 +259,7 @@
     d_out = d_out.astype(bf16)
     zero = jnp.zeros_like(d_out)
     head_of = lax.broadcasted_iota(jnp.int32, (rows, width), 1) // HEAD_DIM
-    product = d_out.astype(f32) * o_ref[...].astype(f32)
+    product = d_out.astype(f32) * (o_ref[...].astype(f32) + rest_ref[...].astype(f32))
     high = product.astype(bf16)
     rest = (product - high.astype(f32)).astype(bf16)
     row_of = lax.broadcasted_iota(jnp.int32, (8, width), 0)
@@ -309,7 +315,7 @@
         sum_ref[2:3, :] += jnp.sum(low_value.astype(f32), axis=0, keepdims=True)
 
 
-def attend_back(after, qkv, attended, cot, first, count, exits, lse, mask, cosine, sine, low, rows):
+def attend_back(after, qkv, attended, rest, cot, first, count, exits, lse, mask, cosine, sine, low, rows):
     pieces, lows = exits
     _, seq_len, model_width = cot.shape
     width = qkv.shape[3]
@@ -327,7 +333,7 @@
         partial(attend_back_kernel, lows, first),
         after,
         low,
-        [qkv, qkv, qkv, attended, cot, lse, mask, cosine, sine, *pieces],
+        [qkv, qkv, qkv, attended, rest, cot, lse, mask, cosine, sine, *pieces],
         [
             jax.ShapeDtypeStruct((count, seq_len, 3 * width), bf16),
             jax.ShapeDtypeStruct((8, width), f32),
@@ -338,6 +344,7 @@
             pl.BlockSpec((None, None, rows, width), lambda s, i, low: (0, first + s, i, 0)),
             pl.BlockSpec((None, None, seq_len, width), lambda s, i, low: (1, first + s, 0, 0)),
             pl.BlockSpec((None, None, seq_len, width), lambda s, i, low: (2, first + s, 0, 0)),
+            rows_of(width),
             rows_of(width),
             rows_of(model_width),
             pl.BlockSpec((None, stat_rows, rows), lambda s, i, low: (first + s, 0, i)),
@@ -424,14 +431,25 @@
     )
 
 
-def back_rows_kernel(entry_lows, exit_lows, tick_ref, g_ref, slope_ref, c_ref, *refs):
+def from_relative(ref, rank, ranks, piece):
+    return jnp.concatenate(
+        [ref[:, pl.ds(pl.multiple_of((rank ^ j) * piece, piece), piece)] for j in range(ranks)], axis=1
+    )
+
+
+def back_rows_kernel(
+    entry_lows, exit_lows, ranks, rank_ref, g_ref, slope_ref, c_ref, x_ref, norm_ref, *refs
+):
     entry, exits = refs[: len(entry_lows)], refs[len(entry_lows) : len(entry_lows) + len(exit_lows)]
-    hidden_ref, normed_ref, sum_ref = refs[-3:]
+    hidden_ref, normed_ref, sum_ref, norm_sum_ref, norm_total = refs[-5:]
     units = slope_ref.shape[1]
-
-    @pl.when((pl.program_id(0) == 0) & (pl.program_id(1) == 0))
+    first = (pl.program_id(0) == 0) & (pl.program_id(1) == 0)
+    final = (pl.program_id(0) == pl.num_programs(0) - 1) & (pl.program_id(1) == pl.num_programs(1) - 1)
+
+    @pl.when(first)
     def _():
         sum_ref[...] = jnp.zeros_like(sum_ref)
+        norm_total[...] = jnp.zeros_like(norm_total)
 
     total = None
     for low, ref in zip(exit_lows, exits):
@@ -441,11 +459,19 @@
     hidden_ref[...] = d_hidden
     sum_ref[0:1, :] += jnp.sum(d_hidden.astype(f32), axis=0, keepdims=True)
     for low, ref in zip(entry_lows, entry):
+        here = slice(low, low + ref.shape[0])
         term = nt(d_hidden, ref[:, :units]) + nt(c_ref[...], ref[:, units:])
-        normed_ref[:, low : low + ref.shape[0]] = term.astype(bf16)
-
-
-def back_rows(after, tick, cot, slope, d_cat, entry, exits, rows):
+        normed_ref[:, here] = term.astype(bf16)
+        unit = (x_ref[:, here].astype(f32) - norm_ref[1:2, here]) * (1.0 / norm_ref[0:1, here])
+        norm_total[0:1, here] += jnp.sum(term * unit, axis=0, keepdims=True)
+        norm_total[1:2, here] += jnp.sum(term, axis=0, keepdims=True)
+
+    @pl.when(final)
+    def _():
+        norm_sum_ref[...] = from_relative(norm_total, rank_ref[0], ranks, norm_total.shape[1] // ranks)
+
+
+def back_rows(after, rank, cot, slope, d_cat, normed, norm_rel, entry, exits, ranks, rows):
     pieces, lows = entry
     exit_pieces, exit_lows = exits
     count, seq_len, model_width = cot.shape
@@ -455,14 +481,15 @@
         return pl.BlockSpec((None, rows, columns), lambda s, i, _: (s, i, 0))
 
     return staged(
-        partial(back_rows_kernel, lows, exit_lows),
+        partial(back_rows_kernel, lows, exit_lows, ranks),
         after,
-        tick,
-        [cot, slope, d_cat, *pieces, *exit_pieces],
+        rank,
+        [cot, slope, d_cat, normed, norm_rel, *pieces, *exit_pieces],
         [
             jax.ShapeDtypeStruct((count, seq_len, units), bf16),
             jax.ShapeDtypeStruct((count, seq_len, model_width), bf16),
             jax.ShapeDtypeStruct((8, units), f32),
+            jax.ShapeDtypeStruct((8, model_width), f32),
         ],
         "back_rows",
         grid=(count, seq_len // rows),
@@ -470,6 +497,8 @@
             rows_of(model_width),
             rows_of(units),
             rows_of(d_cat.shape[2]),
+            rows_of(model_width),
+            resident(norm_rel),
             *[resident(piece) for piece in pieces],
             *[block_of(piece, (units, piece.shape[1]), (0, 0)) for piece in exit_pieces],
         ],
@@ -477,7 +506,9 @@
             rows_of(units),
             rows_of(model_width),
             pl.BlockSpec((8, units), lambda s, i, _: (0, 0)),
-        ],
+            pl.BlockSpec((8, model_width), lambda s, i, _: (0, 0)),
+        ],
+        scratch_shapes=[pltpu.VMEM((8, model_width), f32)],
     )
 
 
@@ -488,70 +519,82 @@
     return [(at * parts, (at + 1) * parts) for at in range(ranks)]
 
 
-def rows_grad_kernel(spans, tick_ref, left, right, *outs):
+def turn_kernel(tick_ref, x_ref, h_ref, a_ref, normed_ref, exit_ref):
+    units = h_ref.shape[1]
+    normed_ref[...] = jnp.transpose(x_ref[...])
+    exit_ref[:units, :] = jnp.transpose(h_ref[...])
+    exit_ref[units:, :] = jnp.transpose(a_ref[...])
+
+
+def turn(after, tick, normed, hidden, attended, rows):
+    tokens, model_width = normed.shape
+    units, width = hidden.shape[1], attended.shape[1]
+
+    def rows_of(columns):
+        return pl.BlockSpec((rows, columns), lambda i, _: (i, 0))
+
+    def columns_of(height):
+        return pl.BlockSpec((height, rows), lambda i, _: (0, i))
+
+    return staged(
+        turn_kernel,
+        after,
+        tick,
+        [normed, hidden, attended],
+        [
+            jax.ShapeDtypeStruct((model_width, tokens), bf16),
+            jax.ShapeDtypeStruct((units + width, tokens), bf16),
+        ],
+        "turn",
+        grid=(tokens // rows,),
+        in_specs=[rows_of(model_width), rows_of(units), rows_of(width)],
+        out_specs=[columns_of(model_width), columns_of(units + width)],
+    )
+
+
+def grad_kernel(spans, tick_ref, left, right, *outs):
     step = pl.program_id(0)
     for (begin, end), out_ref in zip(spans, outs):
 
         @pl.when((step >= begin) & (step < end))
         def _(out_ref=out_ref):
-            out_ref[...] = tn(left[...], right[...]).astype(bf16)
+            out_ref[...] = nn(left[...], right[...]).astype(bf16)
 
 
 def rows_grad(after, tick, left, right, ranks, name):
-    tokens, model_width = left.shape
+    model_width, tokens = left.shape
     columns = right.shape[1]
     piece = model_width // ranks
     parts = max(2, piece // 256)
     block = piece // parts
     spans = targets(ranks, parts)
 
-    def column_block(i, _):
-        return (0, (ranks - 1 - i // parts) * parts + i % parts)
+    def row_block(i, _):
+        return ((ranks - 1 - i // parts) * parts + i % parts, 0)
 
     def target_block(begin, end):
         return lambda i, _: (jnp.clip(i - begin, 0, end - begin - 1), 0)
 
     return staged(
-        partial(rows_grad_kernel, spans),
+        partial(grad_kernel, spans),
         after,
         tick,
         [left, right],
         [jax.ShapeDtypeStruct(((end - begin) * block, columns), bf16) for begin, end in spans],
         name,
         grid=(ranks * parts,),
-        in_specs=[pl.BlockSpec((tokens, block), column_block), resident(right)],
+        in_specs=[pl.BlockSpec((block, tokens), row_block), resident(right)],
         out_specs=[pl.BlockSpec((block, columns), target_block(*span)) for span in spans],
     )
 
 
-def columns_grad_kernel(spans, tick_ref, *refs):
-    kinds = (len(refs) - 1 - len(spans)) // 2
-    left, right, outs, turned = refs[:kinds], refs[kinds], refs[kinds + 1 : -kinds], refs[-kinds:]
-    step = pl.program_id(0)
-
-    @pl.when(step == 0)
-    def _():
-        for source, target in zip(left, turned):
-            target[...] = jnp.transpose(source[...])
-
-    for (begin, end), out_ref in zip(spans, outs):
-
-        @pl.when((step >= begin) & (step < end))
-        def _(out_ref=out_ref):
-            first = 0
-            for kind in range(kinds):
-                total = nn(turned[kind][...], right[...])
-                out_ref[first : first + total.shape[0], :] = total.astype(bf16)
-                first += total.shape[0]
-
-
-def columns_grad(after, tick, lefts, right, ranks, name):
+def columns_grad(after, tick, left, right, ranks, name):
+    height = left.shape[0]
     tokens, model_width = right.shape
     piece = model_width // ranks
     parts = 2
     block = piece // parts
     spans = targets(ranks, parts)
-    height = sum(left.shape[1] for left in lefts)
 
     def column_block(i, _):
         return (0, (ranks - 1 - i // parts) * parts + i % parts)
@@ -560,16 +603,15 @@
         return lambda i, _: (0, jnp.clip(i - begin, 0, end - begin - 1))
 
     return staged(
-        partial(columns_grad_kernel, spans),
+        partial(grad_kernel, spans),
         after,
         tick,
-        [*lefts, right],
+        [left, right],
         [jax.ShapeDtypeStruct((height, (end - begin) * block), bf16) for begin, end in spans],
         name,
         grid=(ranks * parts,),
-        in_specs=[*[resident(left) for left in lefts], pl.BlockSpec((tokens, block), column_block)],
+        in_specs=[resident(left), pl.BlockSpec((tokens, block), column_block)],
         out_specs=[pl.BlockSpec((height, block), target_block(*span)) for span in spans],
-        scratch_shapes=[pltpu.VMEM((left.shape[1], tokens), bf16) for left in lefts],
     )
 
 
@@ -626,51 +668,34 @@
     )
 
 
-def from_relative(ref, rank, ranks, piece):
-    return jnp.concatenate(
-        [ref[:, pl.ds(pl.multiple_of((rank ^ j) * piece, piece), piece)] for j in range(ranks)], axis=1
-    )
-
-
-def input_grad_kernel(ranks, rank_ref, x_ref, g_ref, norm_ref, d_ref, out_ref, sum_ref):
+def input_grad_kernel(ranks, rank_ref, x_ref, g_ref, norm_ref, d_ref, out_ref):
     piece = x_ref.shape[1] // ranks
     inputs = x_ref[...].astype(f32)
     centred = inputs - jnp.mean(inputs, axis=1, keepdims=True)
     variance = jnp.mean(centred * centred, axis=1, keepdims=True)
     inv_std = lax.rsqrt(variance + norm_eps)
     unit = centred * inv_std
-    cot = g_ref[...].astype(f32)
-
-    @pl.when(pl.program_id(0) == 0)
-    def _():
-        sum_ref[...] = jnp.zeros_like(sum_ref)
-
-    d_normed = from_relative(d_ref, rank_ref[0], ranks, piece).astype(f32)
-    d_unit = d_normed * norm_ref[0:1, :]
+    d_unit = from_relative(d_ref, rank_ref[0], ranks, piece).astype(f32) * norm_ref[0:1, :]
     mean_unit = jnp.mean(d_unit, axis=1, keepdims=True)
     mean_cross = jnp.mean(d_unit * unit, axis=1, keepdims=True)
+    cot = g_ref[...].astype(f32)
     out_ref[...] = (cot + inv_std * (d_unit - mean_unit - unit * mean_cross)).astype(bf16)
-    sum_ref[0:1, :] += jnp.sum(d_normed * unit, axis=0, keepdims=True)
-    sum_ref[1:2, :] += jnp.sum(d_normed, axis=0, keepdims=True)
-    sum_ref[2:3, :] += jnp.sum(cot, axis=0, keepdims=True)
 
 
 def input_gradient(after, rank, tokens, cot_rows, norm_params, grads, ranks):
     count, rows, model_width = tokens.shape
-    block = pl.BlockSpec((None, rows, model_width), lambda s, _: (s, 0, 0))
+    part = rows // 2
+    block = pl.BlockSpec((None, part, model_width), lambda s, i, _: (s, i, 0))
     return staged(
         partial(input_grad_kernel, ranks),
         after,
         rank,
         [tokens, cot_rows, norm_params, grads],
-        [
-            jax.ShapeDtypeStruct(tokens.shape, bf16),
-            jax.ShapeDtypeStruct((8, model_width), f32),
-        ],
+        jax.ShapeDtypeStruct(tokens.shape, bf16),
         "input_grad",
-        grid=(count,),
+        grid=(count, rows // part),
         in_specs=[block, block, resident(norm_params), block],
-        out_specs=[block, pl.BlockSpec((8, model_width), lambda s, _: (0, 0))],
+        out_specs=block,
     )
 
 
@@ -715,8 +740,39 @@
 
     def run(self, stage, *arguments):
         result = stage(self.pending, *arguments)
-        self.pending = [jax.tree.leaves(result)[0]]
+        self.pending = [jax.tree.leaves(result)[-1]]
         return result
+
+
+def add_halves_kernel(axis, count, near_ref, far_ref, top_ref, bottom_ref, *refs):
+    near_out, far_out = refs[count:]
+    half = near_ref.shape[axis] // 2
+    first = (slice(0, half), slice(None)) if axis == 0 else (slice(None), slice(0, half))
+    second = (slice(half, None), slice(None)) if axis == 0 else (slice(None), slice(half, None))
+    near_out[first] = near_ref[first]
+    near_out[second] = plus(near_ref[second], bottom_ref[...])
+    far_out[first] = plus(far_ref[first], top_ref[...])
+    far_out[second] = far_ref[second]
+
+
+def add_halves(after, near, far, top, bottom, axis):
+    anywhere = pl.BlockSpec(memory_space=pl.ANY)
+    shape = jax.ShapeDtypeStruct(near.shape, near.dtype)
+    columns = near.shape[1]
+    blocks = 1 if axis == 0 else 2
+    rows = near.shape[0] // blocks
+    whole = pl.BlockSpec((rows, columns), lambda i: (i, 0))
+    part = pl.BlockSpec((top.shape[0] // blocks, top.shape[1]), lambda i: (i, 0))
+    return pl.pallas_call(
+        partial(add_halves_kernel, axis, len(after)),
+        grid=(blocks,),
+        in_specs=[whole, whole, part, part, *[anywhere] * len(after)],
+        out_specs=[whole, whole],
+        out_shape=[shape, shape],
+        compiler_params=pltpu.CompilerParams(vmem_limit_bytes=VMEM * 1024 * 1024),
+        cost_estimate=pl.CostEstimate(flops=10**6, bytes_accessed=10**6, transcendentals=0),
+        name="add_halves",
+    )(near, far, top, bottom, *after)
 
 
 class Gather:
@@ -760,17 +816,22 @@
             self.first = [swap(piece, self.size - 1 - at) for at, piece in enumerate(pieces[:-1])]
 
     def forward(self, after=()):
+        self.sums = []
         if self.size != 4:
             return [self.own, *self.first]
-        top, bottom = hold(self.first, after) if after else self.first
-        half = self.near.shape[self.axis] // 2
-
-        def halves(array):
-            return [lax.slice_in_dim(array, at, at + half, axis=self.axis) for at in (0, half)]
-
-        near, far = halves(self.near), halves(self.far)
-        near = jnp.concatenate([near[0], plus(near[1], bottom)], axis=self.axis)
-        far = jnp.concatenate([plus(far[0], top), far[1]], axis=self.axis)
+        if after:
+            near, far = add_halves(after, self.near, self.far, *self.first, self.axis)
+        else:
+            top, bottom = self.first
+            half = self.near.shape[self.axis] // 2
+
+            def halves(array):
+                return [lax.slice_in_dim(array, at, at + half, axis=self.axis) for at in (0, half)]
+
+            near, far = halves(self.near), halves(self.far)
+            near = jnp.concatenate([near[0], plus(near[1], bottom)], axis=self.axis)
+            far = jnp.concatenate([plus(far[0], top), far[1]], axis=self.axis)
+        self.sums = [near, far]
         return [self.own, swap(near, 1), swap(far, 2)]
 
 
@@ -786,14 +847,11 @@
     return terms[0]
 
 
-def sum_over(array, axis):
+def sum_rounds(axis):
     distances = [1 << bit for bit in range((lax.axis_size(axis) - 1).bit_length())]
-    first = len(distances) % 2
-    if first:
-        array = sum_axis(array, axis, distances[:1])
-    for at in range(first, len(distances), 2):
-        array = sum_axis(array, axis, distances[at : at + 2])
-    return array
+    odd = len(distances) % 2
+    rounds = [distances[:1]] if odd else []
+    return rounds + [distances[at : at + 2] for at in range(odd, len(distances), 2)]
 
 
 def body(
@@ -870,7 +928,7 @@
     units_local = expand_weight.shape[1]
 
     line.wait(mask_columns)
-    qkv, attended, lse = line.run(
+    qkv, attended, rest, lse = line.run(
         attend, normed, 0, count, entry, heads_bias, cosine, sine, mask_rows, lows, rows
     )
     exit_gather.forward([attended])
@@ -886,21 +944,29 @@
     def adam(moments, terms, row=0, column=0, parts=0):
         return line.run(adam_sum, tick, moments, terms, 1.0 / seq_len, row, column, parts)
 
-    exit_parts = line.run(
-        columns_grad, tick, [tokens_of(hidden), tokens_of(attended)], tokens_of(cot), ranks, "exit_grad"
-    )
+    normed_turned, exit_turned = line.run(
+        turn, tick, tokens_of(normed), tokens_of(hidden), tokens_of(attended), rows
+    )
+    exit_parts = line.run(columns_grad, tick, exit_turned, tokens_of(cot), ranks, "exit_grad")
     exit_scatter = Scatter(exit_parts, 1)
     d_cat, bias_sums = line.run(
-        attend_back, qkv, attended, cot, 0, count, exits, lse, mask_columns, cosine, sine, lows, rows
+        attend_back, qkv, attended, rest, cot, 0, count, exits, lse, mask_columns, cosine, sine, lows, rows
     )
     exit_terms = exit_scatter.forward([d_cat])
-    d_hidden, sums, hidden_sums = line.run(back_rows, tick, cot, slope, d_cat, entry, exits, big)
-    grads = scatter_rows(hold([sums], exit_terms[1:])[0])
+    d_hidden, sums, hidden_sums, norm_part = line.run(
+        back_rows, rank_here, cot, slope, d_cat, normed, norm_rel, entry, exits, ranks, big
+    )
+    sums = hold([sums], exit_terms[1:])[0]
+    grads = scatter_rows(sums)
     line.wait(outs)
-    expand_parts = line.run(rows_grad, tick, tokens_of(normed), tokens_of(d_hidden), ranks, "expand_grad")
+    column_sums = jnp.concatenate([norm_part[:2].reshape(-1), jnp.sum(cotangent.astype(f32), axis=(0, 1))])
+    earlier, *later = sum_rounds("tensor")
+    column_sums = sum_axis(column_sums, "tensor", earlier)
+    expand_parts = line.run(rows_grad, tick, normed_turned, tokens_of(d_hidden), ranks, "expand_grad")
     expand_scatter = Scatter(expand_parts, 0)
     expand_terms = expand_scatter.forward()
-    heads_parts = line.run(rows_grad, tick, tokens_of(normed), tokens_of(d_cat), ranks, "heads_grad")
+    line.wait(column_sums)
+    heads_parts = line.run(rows_grad, tick, normed_turned, tokens_of(d_cat), ranks, "heads_grad")
     heads_scatter = Scatter(heads_parts, 0, expand_scatter.first)
     heads_terms = heads_scatter.forward()
     line.wait(*heads_scatter.ends)
@@ -909,14 +975,16 @@
     line.wait(*heads_scatter.first)
     output = line.run(layer_output, rank_here, tokens, output_bias, outs, ranks)
     expand_upd, expand_mom = adam(expand_moments, expand_terms)
-    line.wait(*heads_terms[1:])
-    input_grad, column_sums = line.run(
-        input_gradient, rank_here, tokens, cotangent, norm_params, grads, ranks
-    )
+    for distances in later:
+        column_sums = hold([column_sums], [*heads_terms[1:], expand_upd])[0]
+        column_sums = sum_axis(column_sums, "tensor", distances)
+    input_grad = line.run(input_gradient, rank_here, tokens, cotangent, norm_params, grads, ranks)
+    line.wait(column_sums)
+    totals = jnp.concatenate([column_sums, bias_sums[:3].reshape(-1), hidden_sums[0]])
+    totals = hold([totals], [input_grad])[0]
+    for distances in sum_rounds("dp"):
+        totals = sum_axis(totals, "dp", distances)
     heads_upd, heads_mom = adam(heads_moments, heads_terms, parts=3)
-    column_sums = sum_over(column_sums, "tensor")
-    bias_sums = jnp.concatenate([bias_sums[:3].reshape(-1), hidden_sums[0]])
-    totals = sum_over(jnp.concatenate([column_sums[:3].reshape(-1), bias_sums]), "dp")
     norm_total = totals[: 2 * model_width].reshape(2, model_width)
     output_bias_total = totals[2 * model_width : 3 * model_width]
     bias_total = totals[3 * model_width :]

time: 408 us -> 406 us (level)
  waiting for transfers between devices: 88 us -> 72.7 us
  Pallas kernels: 204 us -> 219 us
    all_gather x2, waiting for transfers between devices: 19.8 us -> 6.59 us  [gather_rows(): return lax.all_gather(array, 'tensor', axis=1, tiled=True)]
    pallas_call x14 -> x15, Pallas kernels: 204 us -> 216 us  [staged(): pl.pallas_call(without, grid_spec=pltpu.PrefetchScalarGridSpec(num_scalar...]
    unnamed x68 -> x73, local copies, waits for them, and re-layouts: 9.98 us -> 11.3 us
  transfers between devices with their start and end apart: 31 -> 31, of which waited for: 11 -> 9; matrix products, arithmetic and copies ran while one was open for 11% -> 10% of each run, Pallas kernels for 49% -> 54%
where the time goes in v1:
time: 406 us; the launch traced here: 400 us
  Pallas kernels  219 us (54%)
  waiting for transfers between devices  72.7 us (18%)
  starting transfers between devices  35.6 us (9%)
  other arithmetic  35.3 us (9%)
  local copies, waits for them, and re-layouts  23.1 us (6%)
  between operations  14.7 us (4%)
    pallas_call x15, Pallas kernels, staged(): pl.pallas_call(without, grid_spec=pltpu.PrefetchScalarGridSpec(num_scalar...  216 us
    ppermute x20, waiting for transfers between devices, swap(): return lax.ppermute(array, 'dp', [(i, i ^ distance) for i in range(size)])  62.8 us
    ppermute x20, starting transfers between devices, swap(): return lax.ppermute(array, 'dp', [(i, i ^ distance) for i in range(size)])  27.4 us
    unnamed x73, local copies, waits for them, and re-layouts  11.3 us
  transfers between devices with their start and end apart: 31, of which 9 were waited for; matrix products, arithmetic and copies ran while one was open for 10% of the time, Pallas kernels for 54%

profile of v1, /device:TPU:0, one launch (start us, length us, event | category | flops | bytes accessed | tf_op | source)
XLA Modules:
  0.0 400.4 jit_solution(4424280896060677264)
XLA Ops:
  14.9 3.0 collective-permute-start
  21.6 1.9 convert.22
  26.5 31.5 %collective-permute-done.refs_9_.refs_10_.refs_11_.refs_4_.refs_7_ = bf16[512,1792]{1,0:T(8,128)(2,1)} collective-permute-done((bf16[512,1792]{1,0:T(8,128)(2,1)S(1)}, bf16[512,1792]{1,0:T(8,128)(2,1)}, u32[]{:S(2)}, u32[]{:S(2)}) %collective-permute-start) | collective-permute-done | bytes 1835040 | tf_op jit(solution)/shard_map/ppermute | solution.py:727
  59.2 1.8 collective-permute-start.2
  63.9 7.2 %select_convert_fusion = (bf16[2,1024,1024]{2,1,0:T(8,128)(2,1)}, bf16[2,1024,1024]{2,1,0:T(8,128)(2,1)}) fusion(s32[2,1024]{1,0:T(2,128)S(1)} %get-tuple-element.159, pred[1024,1024]{1,0:T(8,128)(4,1)S(1)} %get-tuple-element.167, pred[2,1024]{1,0:T(4,128)(4,1)S(1)} %broadcast_compare_fusion, pred[1024,1024]{1,0:T(8,128)(4,1)S(1)} %get-tuple-element.168, ...), kind=kLoop, calls=%fused_computation | loop fusion | flops 25165824 | bytes 12593152 | tf_op jit(solution)/shard_map/vmap()/convert_element_type | solution.py:52
  71.1 9.8 %collective-permute-done.2.refs_15_.refs_16_.refs_17_.refs_6_.refs_1_.refs_9_ = bf16[256,1792]{1,0:T(8,128)(2,1)S(1)} collective-permute-done((bf16[256,1792]{1,0:T(8,128)(2,1)S(1)}, bf16[256,1792]{1,0:T(8,128)(2,1)S(1)}, u32[]{:S(2)}, u32[]{:S(2)}) %collective-permute-start.2) | collective-permute-done | bytes 917536 | tf_op jit(solution)/shard_map/ppermute | solution.py:727
  80.9 2.5 collective-permute-done.3.refs_18_.refs_19_.refs_20_.refs_7_.refs_2_.refs_10_
  86.3 5.5 %fusion.10 = (f32[2,1024,128]{2,1,0:T(8,128)}, f32[2,1024,128]{2,1,0:T(8,128)}) fusion(f32[128]{0:T(128)S(1)} %compare_select_fusion, f32[128]{0:T(128)S(1)} %mul.306, f32[2,1024]{1,0:T(2,128)S(1)} %get-tuple-element.158), kind=kLoop, calls=%fused_computation.25 | loop fusion | flops 524288 | bytes 2106368 | tf_op jit(solution)/shard_map/vmap()/mul | solution.py:44
  91.8 4.3 %all-gather.3.cloned.1.call-done.refs_1_.refs_4_ = bf16[2,1024,2048]{2,1,0:T(8,128)(2,1)} async-done(((bf16[2,128,2048]{2,1,0:T(8,128)(2,1)}), bf16[2,1024,2048]{2,1,0:T(8,128)(2,1)}) %all-gather.3.cloned.1.call-update) | async-done | bytes 8388624 | tf_op jit(solution)/shard_map/all_gather | solution.py:905
  96.1 23.2 %attend.1 = (bf16[3,2,1024,256]{3,2,1,0:T(8,128)(2,1)}, bf16[2,1024,256]{2,1,0:T(8,128)(2,1)}, bf16[2,1024,256]{2,1,0:T(8,128)(2,1)}, f32[2,8,1024]{2,1,0:T(8,128)}) custom-call(s32[2,4]{1,0:T(2,128)} %and_select_fusion.1.first_ref, bf16[2,1024,1024]{2,1,0:T(8,128)(2,1)} %get-tuple-element.153.refs_0_.refs_8_, ...), custom_call_target="tpu_custom_call" | custom-call | flops 10000000000 | bytes 10000000 | tf_op jit(solution)/shard_map/attend/pallas_call | solution.py:103
  122.0 2.5 collective-permute-start.6
  127.2 17.6 %gelu_units.1 = (bf16[2,1024,1024]{2,1,0:T(8,128)(2,1)}, bf16[2,1024,1024]{2,1,0:T(8,128)(2,1)}) custom-call(s32[1]{0:T(128)} %bitcast.1.first_ref, f32[2,8,1024]{2,1,0:T(8,128)} %get-tuple-element.61.refs_0_.refs_7_, bf16[2,1024,2048]{2,1,0:T(8,128)(2,1)} %all-gather.3.cloned.1.call-done.refs_1_.refs_4_, f32[1,1024]{1,0:T(1,128)} %bitcast.106, ...), custom_call_target="tpu_custom_call" | custom-call | flops 10000000000 | bytes 10000000 | tf_op jit(solution)/shard_map/gelu_units/pallas_call | solution.py:103
  145.9 17.0 %out_sums.1.refs_0_ = bf16[2,1024,2048]{2,1,0:T(8,128)(2,1)} custom-call(s32[1]{0:T(128)} %bitcast.1.first_ref, bf16[2,1024,1024]{2,1,0:T(8,128)(2,1)} %get-tuple-element.62.refs_0_.refs_2_, bf16[2,1024,256]{2,1,0:T(8,128)(2,1)} %get-tuple-element.63.refs_2_.refs_1_.refs_4_, bf16[2,1024,1024]{2,1,0:T(8,128)(2,1)} %get-tuple-element.64.refs_2_, ...), custom_call_target="tpu_custom_call" | custom-call | flops 10000000000 | bytes 10000000 | tf_op jit(solution)/shard_map/out_sums/pallas_call | solution.py:103
  163.0 13.1 %turn.1 = (bf16[2048,2048]{1,0:T(8,128)(2,1)}, bf16[1280,2048]{1,0:T(8,128)(2,1)}) custom-call(s32[1]{0:T(128)} %bitcast.1.first_ref, bf16[2,1024,2048]{2,1,0:T(8,128)(2,1)} %out_sums.1.refs_0_, bf16[2048,2048]{1,0:T(8,128)(2,1)} %bitcast.89, bf16[2048,1024]{1,0:T(8,128)(2,1)} %bitcast.108, bf16[2048,256]{1,0:T(8,128)(2,1)} %bitcast.91), custom_call_target="tpu_custom_call" | custom-call | flops 10000000000 | bytes 10000000 | tf_op jit(solution)/shard_map/turn/pallas_call | solution.py:103
  176.1 2.2 all-gather.5.cloned.1.call-done.refs_6_.refs_1_
  178.4 18.2 %exit_grad.1 = (bf16[1280,256]{1,0:T(8,128)(2,1)}, bf16[1280,256]{1,0:T(8,128)(2,1)}, bf16[1280,512]{1,0:T(8,128)(2,1)}, bf16[1280,512]{1,0:T(8,128)(2,1)}, bf16[1280,512]{1,0:T(8,128)(2,1)}) custom-call(s32[1]{0:T(128)} %bitcast.1.first_ref, bf16[1280,2048]{1,0:T(8,128)(2,1)} %get-tuple-element.67.refs_0_.refs_1_, ...), custom_call_target="tpu_custom_call" | custom-call | flops 10000000000 | bytes 10000000 | tf_op jit(solution)/shard_map/exit_grad/pallas_call | solution.py:103
  199.6 31.4 %attend_back.1 = (bf16[2,1024,768]{2,1,0:T(8,128)(2,1)}, f32[8,256]{1,0:T(8,128)}) custom-call(s32[2,4]{1,0:T(2,128)} %and_select_fusion.1.first_ref, bf16[1280,512]{1,0:T(8,128)(2,1)} %get-tuple-element.68.refs_0_.refs_4_.refs_2_, bf16[3,2,1024,256]{3,2,1,0:T(8,128)(2,1)} %get-tuple-element.69.refs_1_.refs_2_.refs_3_, ...), custom_call_target="tpu_custom_call" | custom-call | flops 10000000000 | bytes 10000000 | tf_op jit(solution)/shard_map/attend_back/pallas_call | solution.py:103
  232.0 3.3 add_halves.1
  237.5 33.6 %back_rows.1 = (bf16[2,1024,1024]{2,1,0:T(8,128)(2,1)}, bf16[2,1024,2048]{2,1,0:T(8,128)(2,1)}, f32[8,1024]{1,0:T(8,128)}, f32[8,2048]{1,0:T(8,128)}) custom-call(s32[1]{0:T(128)} %bitcast.first_ref, f32[8,256]{1,0:T(8,128)} %get-tuple-element.71.refs_0_, bf16[2,1024,2048]{2,1,0:T(8,128)(2,1)} %all-gather.5.cloned.1.call-done.refs_6_.refs_1_, ...), custom_call_target="tpu_custom_call" | custom-call | flops 10000000000 | bytes 10000000 | tf_op jit(solution)/shard_map/back_rows/pallas_call | solution.py:103
  276.7 15.5 %expand_grad.1 = (bf16[256,1024]{1,0:T(8,128)(2,1)}, bf16[256,1024]{1,0:T(8,128)(2,1)}, bf16[512,1024]{1,0:T(8,128)(2,1)}, bf16[512,1024]{1,0:T(8,128)(2,1)}, bf16[512,1024]{1,0:T(8,128)(2,1)}) custom-call(s32[1]{0:T(128)} %bitcast.1.first_ref, f32[8,2048]{1,0:T(8,128)} %get-tuple-element.73.refs_0_, ...), custom_call_target="tpu_custom_call" | custom-call | flops 10000000000 | bytes 10000000 | tf_op jit(solution)/shard_map/expand_grad/pallas_call | solution.py:103
  294.4 13.7 %heads_grad.1 = (bf16[256,768]{1,0:T(8,128)(2,1)}, bf16[256,768]{1,0:T(8,128)(2,1)}, bf16[512,768]{1,0:T(8,128)(2,1)}, bf16[512,768]{1,0:T(8,128)(2,1)}, bf16[512,768]{1,0:T(8,128)(2,1)}) custom-call(s32[1]{0:T(128)} %bitcast.1.first_ref, bf16[512,1024]{1,0:T(8,128)(2,1)} %get-tuple-element.76.refs_0_.refs_2_, f32[6144]{0:T(1024)} %fusion.33.refs_1_.refs_0_, ...), custom_call_target="tpu_custom_call" | custom-call | flops 10000000000 | bytes 10000000 | tf_op jit(solution)/shard_map/heads_grad/pallas_call | solution.py:103
  319.2 7.6 %adam_sum.4 = (f32[1024,512]{1,0:T(8,128)}, f32[2,1024,512]{2,1,0:T(8,128)}) custom-call(s32[1]{0:T(128)} %bitcast.1.first_ref, bf16[512,768]{1,0:T(8,128)(2,1)} %get-tuple-element.77.refs_0_.refs_3_, bf16[256,768]{1,0:T(8,128)(2,1)} %get-tuple-element.82.refs_1_, bf16[256,768]{1,0:T(8,128)(2,1)} %get-tuple-element.83.refs_2_, f32[2,1024,512]{2,1,0:T(8,128)} %refs_3_.3, ...), custom_call_target="tpu_custom_call" | custom-call | flops 10000000000 | bytes 10000000 | tf_op jit(solution)/shard_map/adam_sum/pallas_call | solution.py:103
  326.8 3.7 adam_sum.5
  334.7 2.5 layer_output.1.refs_0_
  337.3 10.6 %collective-permute-done.18.refs_4_ = bf16[512,1024]{1,0:T(8,128)(2,1)} collective-permute-done((bf16[512,1024]{1,0:T(8,128)(2,1)S(1)}, bf16[512,1024]{1,0:T(8,128)(2,1)}, u32[]{:S(2)}, u32[]{:S(2)}) %collective-permute-start.18) | collective-permute-done | bytes 1048608 | tf_op jit(solution)/shard_map/ppermute | solution.py:727
  347.9 6.6 %adam_sum.6 = (f32[512,1024]{1,0:T(8,128)}, f32[2,512,1024]{2,1,0:T(8,128)}) custom-call(s32[1]{0:T(128)} %bitcast.1.first_ref, bf16[2,128,2048]{2,1,0:T(8,128)(2,1)} %layer_output.1.refs_0_, f32[2,512,1024]{2,1,0:T(8,128)} %refs_1_.4, bf16[512,1024]{1,0:T(8,128)(2,1)} %get-tuple-element.76.refs_0_.refs_2_, ...), custom_call_target="tpu_custom_call" | custom-call | flops 10000000000 | bytes 10000000 | tf_op jit(solution)/shard_map/adam_sum/pallas_call | solution.py:103
  354.5 8.4 %collective-permute-done.20.refs_2_.refs_5_ = bf16[512,768]{1,0:T(8,128)(2,1)S(1)} collective-permute-done((bf16[512,768]{1,0:T(8,128)(2,1)}, bf16[512,768]{1,0:T(8,128)(2,1)S(1)}, u32[]{:S(2)}, u32[]{:S(2)}) %collective-permute-start.20) | collective-permute-done | bytes 786464 | tf_op jit(solution)/shard_map/ppermute | solution.py:727
  365.5 2.9 collective-permute-start.23
  369.3 2.1 collective-permute-done.23
  372.7 4.7 %input_grad.1.refs_1_.refs_0_ = bf16[2,128,2048]{2,1,0:T(8,128)(2,1)} custom-call(s32[1]{0:T(128)} %bitcast.first_ref, f32[2,512,1024]{2,1,0:T(8,128)} %get-tuple-element.115.refs_0_, bf16[2,128,2048]{2,1,0:T(8,128)(2,1)} %refs_1_.5, bf16[2,128,2048]{2,1,0:T(8,128)(2,1)} %refs_2_.4, f32[2,2048]{1,0:T(2,128)} %refs_3_.5, ...), custom_call_target="tpu_custom_call" | custom-call | flops 10000000000 | bytes 10000000 | tf_op jit(solution)/shard_map/input_grad/pallas_call | solution.py:103
  379.2 1.7 collective-permute-start.25
  381.0 7.3 %adam_sum.7 = (f32[3,512,256]{2,1,0:T(8,128)}, f32[2,3,512,256]{3,2,1,0:T(8,128)}) custom-call(s32[1]{0:T(128)} %bitcast.1.first_ref, bf16[2,128,2048]{2,1,0:T(8,128)(2,1)} %input_grad.1.refs_1_.refs_0_, f32[6144]{0:T(1024)} %copy-done.25, f32[2,3,512,256]{3,2,1,0:T(8,128)} %refs_2_.5, bf16[512,768]{1,0:T(8,128)(2,1)} %get-tuple-element.77.refs_0_.refs_3_, ...), custom_call_target="tpu_custom_call" | custom-call | flops 10000000000 | bytes 10000000 | tf_op jit(solution)/shard_map/adam_sum/pallas_call | solution.py:103
  (219 shorter events, 68.7 us)
Async XLA Ops:
  7.2 88.9 %all-gather.3.cloned.1.call-start = ((), (), s32[]{:S(2)}) async-start(), calls=%async_computation.2 | async-start | bytes 9437184 | tf_op jit(solution)/shard_map/all_gather | solution.py:905
  11.2 167.1 %all-gather.5.cloned.1.call-start = ((), (), s32[]{:S(2)}) async-start(), calls=%async_computation.3 | async-start | bytes 9437184 | tf_op jit(solution)/shard_map/all_gather | solution.py:905
  12.4 264.3 %reduce-scatter.3.cloned.1.call-start = ((), (), s32[]{:S(2)}) async-start(), calls=%async_computation.4 | async-start | bytes 9437184 | tf_op jit(solution)/shard_map/reduce_scatter | solution.py:908
  14.9 43.1 %collective-permute-start = (bf16[512,1792]{1,0:T(8,128)(2,1)S(1)}, bf16[512,1792]{1,0:T(8,128)(2,1)}, u32[]{:S(2)}, u32[]{:S(2)}) collective-permute-start(bf16[512,1792]{1,0:T(8,128)(2,1)S(1)} %pad_maximum_fusion.refs_6_.refs_7_.refs_8_.refs_3_), channel_id=1, source_target_pairs={{0,8},{8,0},{16,24},{24,16},{1,9},{9,1},{17,25},{25,17},{2,10},{10... | collective-permute-start | bytes 5505032 | tf_op jit(solution)/shard_map/ppermute | solution.py:727
  17.9 43.2 %collective-permute-start.1 = (bf16[512,1792]{1,0:T(8,128)(2,1)S(1)}, bf16[512,1792]{1,0:T(8,128)(2,1)}, u32[]{:S(2)}, u32[]{:S(2)}) collective-permute-start(bf16[512,1792]{1,0:T(8,128)(2,1)S(1)} %pad_maximum_fusion.refs_6_.refs_7_.refs_8_.refs_3_), channel_id=1, source_target_pairs={{0,16},{8,24},{16,0},{24,8},{1,17},{9,25},{17,1},{25,9},{2,18},{10... | collective-permute-start | bytes 5505032 | tf_op jit(solution)/shard_map/ppermute | solution.py:727
  59.2 21.6 %collective-permute-start.2 = (bf16[256,1792]{1,0:T(8,128)(2,1)S(1)}, bf16[256,1792]{1,0:T(8,128)(2,1)S(1)}, u32[]{:S(2)}, u32[]{:S(2)}) collective-permute-start(bf16[256,1792]{1,0:T(8,128)(2,1)S(1)} %slice.201), channel_id=1, source_target_pairs={{0,16},{8,24},{16,0},{24,8},{1,17},{9,25},{17,1},{25,9},{2,18},{10... | collective-permute-start | bytes 2752520 | tf_op jit(solution)/shard_map/ppermute | solution.py:727
  62.3 21.0 %collective-permute-start.3 = (bf16[256,1792]{1,0:T(8,128)(2,1)S(1)}, bf16[256,1792]{1,0:T(8,128)(2,1)S(1)}, u32[]{:S(2)}, u32[]{:S(2)}) collective-permute-start(bf16[256,1792]{1,0:T(8,128)(2,1)S(1)} %slice.202), channel_id=1, source_target_pairs={{0,8},{8,0},{16,24},{24,16},{1,9},{9,1},{17,25},{25,17},{2,10},{10... | collective-permute-start | bytes 2752520 | tf_op jit(solution)/shard_map/ppermute | solution.py:727
  84.3 35.1 %collective-permute-start.4 = (bf16[1280,512]{1,0:T(8,128)(2,1)}, bf16[1280,512]{1,0:T(8,128)(2,1)S(1)}, u32[]{:S(2)}, u32[]{:S(2)}) collective-permute-start(bf16[1280,512]{1,0:T(8,128)(2,1)} %hold.6.refs_3_.refs_11_), channel_id=1, source_target_pairs={{0,8},{8,0},{16,24},{24,16},{1,9},{9,1},{17,25},{25,17},{2,10},{10... | collective-permute-start | bytes 3932168 | tf_op jit(solution)/shard_map/ppermute | solution.py:727
  85.8 33.6 %collective-permute-start.5 = (bf16[1280,512]{1,0:T(8,128)(2,1)}, bf16[1280,512]{1,0:T(8,128)(2,1)S(1)}, u32[]{:S(2)}, u32[]{:S(2)}) collective-permute-start(bf16[1280,512]{1,0:T(8,128)(2,1)} %hold.6.refs_3_.refs_11_), channel_id=1, source_target_pairs={{0,16},{8,24},{16,0},{24,8},{1,17},{9,25},{17,1},{25,9},{2,18},{10... | collective-permute-start | bytes 3932168 | tf_op jit(solution)/shard_map/ppermute | solution.py:727
  122.0 22.8 %collective-permute-start.6 = (bf16[1280,256]{1,0:T(8,128)(2,1)S(1)}, bf16[1280,256]{1,0:T(8,128)(2,1)S(1)}, u32[]{:S(2)}, u32[]{:S(2)}) collective-permute-start(bf16[1280,256]{1,0:T(8,128)(2,1)S(1)} %slice.169), channel_id=1, source_target_pairs={{0,16},{8,24},{16,0},{24,8},{1,17},{9,25},{17,1},{25,9},{2,18},{10... | collective-permute-start | bytes 1966088 | tf_op jit(solution)/shard_map/ppermute | solution.py:727
  125.6 19.2 %collective-permute-start.7 = (bf16[1280,256]{1,0:T(8,128)(2,1)S(1)}, bf16[1280,256]{1,0:T(8,128)(2,1)S(1)}, u32[]{:S(2)}, u32[]{:S(2)}) collective-permute-start(bf16[1280,256]{1,0:T(8,128)(2,1)S(1)} %slice.170), channel_id=1, source_target_pairs={{0,8},{8,0},{16,24},{24,16},{1,9},{9,1},{17,25},{25,17},{2,10},{10... | collective-permute-start | bytes 1966088 | tf_op jit(solution)/shard_map/ppermute | solution.py:727
  163.0 209.7 %reduce-scatter.5.cloned.1.call-start = ((), (), s32[]{:S(2)}) async-start(), calls=%async_computation.5 | async-start | bytes 9437184 | tf_op jit(solution)/shard_map/reduce_scatter | solution.py:908
  196.6 34.3 %collective-permute-start.11 = (bf16[1280,256]{1,0:T(8,128)(2,1)}, bf16[1280,256]{1,0:T(8,128)(2,1)S(1)}, u32[]{:S(2)}, u32[]{:S(2)}) collective-permute-start(bf16[1280,256]{1,0:T(8,128)(2,1)} %get-tuple-element.86), channel_id=1, source_target_pairs={{0,8},{8,0},{16,24},{24,16},{1,9},{9,1},{17,25},{25,17},{2,10},{10... | collective-permute-start | bytes 1966088 | tf_op jit(solution)/shard_map/ppermute | solution.py:727
  198.1 32.9 %collective-permute-start.12 = (bf16[1280,256]{1,0:T(8,128)(2,1)}, bf16[1280,256]{1,0:T(8,128)(2,1)S(1)}, u32[]{:S(2)}, u32[]{:S(2)}) collective-permute-start(bf16[1280,256]{1,0:T(8,128)(2,1)} %get-tuple-element.87), channel_id=1, source_target_pairs={{0,16},{8,24},{16,0},{24,8},{1,17},{9,25},{17,1},{25,9},{2,18},{10... | collective-permute-start | bytes 1966088 | tf_op jit(solution)/shard_map/ppermute | solution.py:727
  235.3 35.8 %collective-permute-start.13 = (bf16[1280,512]{1,0:T(8,128)(2,1)}, bf16[1280,512]{1,0:T(8,128)(2,1)S(1)}, u32[]{:S(2)}, u32[]{:S(2)}) collective-permute-start(bf16[1280,512]{1,0:T(8,128)(2,1)} %get-tuple-element.88), channel_id=1, source_target_pairs={{0,8},{8,0},{16,24},{24,16},{1,9},{9,1},{17,25},{25,17},{2,10},{10... | collective-permute-start | bytes 3932168 | tf_op jit(solution)/shard_map/ppermute | solution.py:727
  235.9 35.2 %collective-permute-start.14 = (bf16[1280,512]{1,0:T(8,128)(2,1)}, bf16[1280,512]{1,0:T(8,128)(2,1)S(1)}, u32[]{:S(2)}, u32[]{:S(2)}) collective-permute-start(bf16[1280,512]{1,0:T(8,128)(2,1)} %get-tuple-element.89), channel_id=1, source_target_pairs={{0,16},{8,24},{16,0},{24,8},{1,17},{9,25},{17,1},{25,9},{2,18},{10... | collective-permute-start | bytes 3932168 | tf_op jit(solution)/shard_map/ppermute | solution.py:727
  274.8 1.3 collective-permute-start.8
  292.2 19.2 %collective-permute-start.10 = (bf16[256,1024]{1,0:T(8,128)(2,1)}, bf16[256,1024]{1,0:T(8,128)(2,1)S(1)}, u32[]{:S(2)}, u32[]{:S(2)}) collective-permute-start(bf16[256,1024]{1,0:T(8,128)(2,1)} %get-tuple-element.81), channel_id=1, source_target_pairs={{0,16},{8,24},{16,0},{24,8},{1,17},{9,25},{17,1},{25,9},{2,18},{10... | collective-permute-start | bytes 1572872 | tf_op jit(solution)/shard_map/ppermute | solution.py:727
  293.0 18.4 %collective-permute-start.9 = (bf16[256,1024]{1,0:T(8,128)(2,1)}, bf16[256,1024]{1,0:T(8,128)(2,1)S(1)}, u32[]{:S(2)}, u32[]{:S(2)}) collective-permute-start(bf16[256,1024]{1,0:T(8,128)(2,1)} %get-tuple-element.80), channel_id=1, source_target_pairs={{0,8},{8,0},{16,24},{24,16},{1,9},{9,1},{17,25},{25,17},{2,10},{10... | collective-permute-start | bytes 1572872 | tf_op jit(solution)/shard_map/ppermute | solution.py:727
  312.4 18.1 %collective-permute-start.15 = (bf16[256,768]{1,0:T(8,128)(2,1)}, bf16[256,768]{1,0:T(8,128)(2,1)S(1)}, u32[]{:S(2)}, u32[]{:S(2)}) collective-permute-start(bf16[256,768]{1,0:T(8,128)(2,1)} %get-tuple-element.82.refs_1_), channel_id=1, source_target_pairs={{0,8},{8,0},{16,24},{24,16},{1,9},{9,1},{17,25},{25,17},{2,10},{10... | collective-permute-start | bytes 1179656 | tf_op jit(solution)/shard_map/ppermute | solution.py:727
  313.1 19.9 %collective-permute-start.16 = (bf16[256,768]{1,0:T(8,128)(2,1)}, bf16[256,768]{1,0:T(8,128)(2,1)}, u32[]{:S(2)}, u32[]{:S(2)}) collective-permute-start(bf16[256,768]{1,0:T(8,128)(2,1)} %get-tuple-element.83.refs_2_), channel_id=1, source_target_pairs={{0,16},{8,24},{16,0},{24,8},{1,17},{9,25},{17,1},{25,9},{2,18},{10... | collective-permute-start | bytes 1179656 | tf_op jit(solution)/shard_map/ppermute | solution.py:727
  315.8 32.1 %collective-permute-start.18 = (bf16[512,1024]{1,0:T(8,128)(2,1)S(1)}, bf16[512,1024]{1,0:T(8,128)(2,1)}, u32[]{:S(2)}, u32[]{:S(2)}) collective-permute-start(bf16[512,1024]{1,0:T(8,128)(2,1)S(1)} %pad_maximum_fusion.5), channel_id=1, source_target_pairs={{0,16},{8,24},{16,0},{24,8},{1,17},{9,25},{17,1},{25,9},{2,18},{10... | collective-permute-start | bytes 3145736 | tf_op jit(solution)/shard_map/ppermute | solution.py:727
  317.9 30.0 %collective-permute-start.17 = (bf16[512,1024]{1,0:T(8,128)(2,1)}, bf16[512,1024]{1,0:T(8,128)(2,1)}, u32[]{:S(2)}, u32[]{:S(2)}) collective-permute-start(bf16[512,1024]{1,0:T(8,128)(2,1)} %pad_maximum_fusion.4), channel_id=1, source_target_pairs={{0,8},{8,0},{16,24},{24,16},{1,9},{9,1},{17,25},{25,17},{2,10},{10... | collective-permute-start | bytes 3145736 | tf_op jit(solution)/shard_map/ppermute | solution.py:727
  331.6 31.3 %collective-permute-start.20 = (bf16[512,768]{1,0:T(8,128)(2,1)}, bf16[512,768]{1,0:T(8,128)(2,1)S(1)}, u32[]{:S(2)}, u32[]{:S(2)}) collective-permute-start(bf16[512,768]{1,0:T(8,128)(2,1)} %pad_maximum_fusion.7), channel_id=1, source_target_pairs={{0,16},{8,24},{16,0},{24,8},{1,17},{9,25},{17,1},{25,9},{2,18},{10... | collective-permute-start | bytes 2359304 | tf_op jit(solution)/shard_map/ppermute | solution.py:727
  334.1 28.8 %collective-permute-start.19 = (bf16[512,768]{1,0:T(8,128)(2,1)S(1)}, bf16[512,768]{1,0:T(8,128)(2,1)S(1)}, u32[]{:S(2)}, u32[]{:S(2)}) collective-permute-start(bf16[512,768]{1,0:T(8,128)(2,1)S(1)} %pad_maximum_fusion.6), channel_id=1, source_target_pairs={{0,8},{8,0},{16,24},{24,16},{1,9},{9,1},{17,25},{25,17},{2,10},{10... | collective-permute-start | bytes 2359304 | tf_op jit(solution)/shard_map/ppermute | solution.py:727
  364.0 5.2 %collective-permute-start.21 = (f32[6144]{0:T(1024)}, f32[6144]{0:T(1024)S(1)}, u32[]{:S(2)}, u32[]{:S(2)}) collective-permute-start(f32[6144]{0:T(1024)} %hold.10), channel_id=1, source_target_pairs={{0,2},{1,3},{2,0},{3,1},{4,6},{5,7},{6,4},{7,5},{8,10},{9,11},{10,... | collective-permute-start | bytes 73736 | tf_op jit(solution)/shard_map/ppermute | solution.py:843
  364.0 5.2 %collective-permute-start.22 = (f32[6144]{0:T(1024)}, f32[6144]{0:T(1024)S(1)}, u32[]{:S(2)}, u32[]{:S(2)}) collective-permute-start(f32[6144]{0:T(1024)} %hold.10), channel_id=1, source_target_pairs={{0,4},{1,5},{2,6},{3,7},{4,0},{5,1},{6,2},{7,3},{8,12},{9,13},{10,... | collective-permute-start | bytes 73736 | tf_op jit(solution)/shard_map/ppermute | solution.py:843
  365.5 5.8 %collective-permute-start.23 = (f32[6144]{0:T(1024)}, f32[6144]{0:T(1024)S(1)}, u32[]{:S(2)}, u32[]{:S(2)}) collective-permute-start(f32[6144]{0:T(1024)} %hold.10), channel_id=1, source_target_pairs={{0,6},{1,7},{2,4},{3,5},{4,2},{5,3},{6,0},{7,1},{8,14},{9,15},{10,... | collective-permute-start | bytes 73736 | tf_op jit(solution)/shard_map/ppermute | solution.py:843
  377.4 14.8 %copy-start.23 = (f32[2,2,2048]{2,1,0:T(2,128)S(1)}, f32[2,2,2048]{2,1,0:T(2,128)}, u32[]{:S(2)}) copy-start(f32[2,2,2048]{2,1,0:T(2,128)} %param.25) | copy-start | bytes 98308
  377.4 10.8 %collective-permute-start.24 = (f32[7936]{0:T(1024)}, f32[7936]{0:T(1024)S(1)}, u32[]{:S(2)}, u32[]{:S(2)}) collective-permute-start(f32[7936]{0:T(1024)} %hold.11), channel_id=1, source_target_pairs={{0,8},{8,0},{16,24},{24,16},{1,9},{9,1},{17,25},{25,17},{2,10},{10... | collective-permute-start | bytes 95240 | tf_op jit(solution)/shard_map/ppermute | solution.py:843
  379.2 9.1 %collective-permute-start.25 = (f32[7936]{0:T(1024)}, f32[7936]{0:T(1024)S(1)}, u32[]{:S(2)}, u32[]{:S(2)}) collective-permute-start(f32[7936]{0:T(1024)} %hold.11), channel_id=1, source_target_pairs={{0,16},{8,24},{16,0},{24,8},{1,17},{9,25},{17,1},{25,9},{2,18},{10... | collective-permute-start | bytes 95240 | tf_op jit(solution)/shard_map/ppermute | solution.py:843
  380.9 7.4 %collective-permute-start.26 = (f32[7936]{0:T(1024)}, f32[7936]{0:T(1024)S(1)}, u32[]{:S(2)}, u32[]{:S(2)}) collective-permute-start(f32[7936]{0:T(1024)} %hold.11), channel_id=1, source_target_pairs={{0,24},{8,16},{16,8},{24,0},{1,25},{9,17},{17,9},{25,1},{2,26},{10... | collective-permute-start | bytes 95240 | tf_op jit(solution)/shard_map/ppermute | solution.py:843
  (34 other events, 137.2 us)
Sparse Core Ops, SparseCore 0:
  11.3 84.7 all-gather.2
  97.7 80.5 all-gather.4
  180.7 88.1 reduce-scatter.2
  272.7 87.2 reduce-scatter.4

commit v2 on v1

--- a/solution.py
+++ b/solution.py
@@ -975,13 +975,11 @@
     line.wait(*heads_scatter.first)
     output = line.run(layer_output, rank_here, tokens, output_bias, outs, ranks)
     expand_upd, expand_mom = adam(expand_moments, expand_terms)
+    input_grad = line.run(input_gradient, rank_here, tokens, cotangent, norm_params, grads, ranks)
+    (column_sums,) = hold([column_sums], [input_grad])
     for distances in later:
-        column_sums = hold([column_sums], [*heads_terms[1:], expand_upd])[0]
         column_sums = sum_axis(column_sums, "tensor", distances)
-    input_grad = line.run(input_gradient, rank_here, tokens, cotangent, norm_params, grads, ranks)
-    line.wait(column_sums)
     totals = jnp.concatenate([column_sums, bias_sums[:3].reshape(-1), hidden_sums[0]])
-    totals = hold([totals], [input_grad])[0]
     for distances in sum_rounds("dp"):
         totals = sum_axis(totals, "dp", distances)
     heads_upd, heads_mom = adam(heads_moments, heads_terms, parts=3)

time: 406 us -> 404 us (level)
    unnamed x73 -> x67, local copies, waits for them, and re-layouts: 11.3 us -> 11.3 us
  transfers between devices with their start and end apart: 31 -> 31, of which waited for: 9 -> 8; matrix products, arithmetic and copies ran while one was open for 10% -> 9% of each run, Pallas kernels for 54% -> 55%
where the time goes in v2:
time: 404 us; the launch traced here: 397 us
  Pallas kernels  219 us (54%)
  waiting for transfers between devices  73.3 us (18%)
  starting transfers between devices  35.5 us (9%)
  other arithmetic  34.4 us (9%)
  local copies, waits for them, and re-layouts  20 us (5%)
  between operations  14.7 us (4%)
    pallas_call x15, Pallas kernels, staged(): pl.pallas_call(without, grid_spec=pltpu.PrefetchScalarGridSpec(num_scalar...  216 us
    ppermute x20, waiting for transfers between devices, swap(): return lax.ppermute(array, 'dp', [(i, i ^ distance) for i in range(size)])  61.9 us
    ppermute x20, starting transfers between devices, swap(): return lax.ppermute(array, 'dp', [(i, i ^ distance) for i in range(size)])  27.3 us
    unnamed x67, local copies, waits for them, and re-layouts  11.3 us
  transfers between devices with their start and end apart: 31, of which 8 were waited for; matrix products, arithmetic and copies ran while one was open for 9% of the time, Pallas kernels for 55%

profile of v2, /device:TPU:0, one launch (start us, length us, event | category | flops | bytes accessed | tf_op | source)
XLA Modules:
  0.0 397.4 jit_solution(3917664943297156594)
XLA Ops:
  7.3 1.7 constant_dynamic-slice_fusion.3
  14.9 3.0 collective-permute-start
  21.6 1.9 convert.22
  26.5 31.5 %collective-permute-done.refs_9_.refs_10_.refs_11_.refs_4_.refs_7_ = bf16[512,1792]{1,0:T(8,128)(2,1)} collective-permute-done((bf16[512,1792]{1,0:T(8,128)(2,1)S(1)}, bf16[512,1792]{1,0:T(8,128)(2,1)}, u32[]{:S(2)}, u32[]{:S(2)}) %collective-permute-start) | collective-permute-done | bytes 1835040 | tf_op jit(solution)/shard_map/ppermute | solution.py:727
  59.3 1.8 collective-permute-start.2
  63.9 7.2 %select_convert_fusion = (bf16[2,1024,1024]{2,1,0:T(8,128)(2,1)}, bf16[2,1024,1024]{2,1,0:T(8,128)(2,1)}) fusion(s32[2,1024]{1,0:T(2,128)S(1)} %get-tuple-element.159, pred[1024,1024]{1,0:T(8,128)(4,1)S(1)} %get-tuple-element.167, pred[2,1024]{1,0:T(4,128)(4,1)S(1)} %broadcast_compare_fusion, pred[1024,1024]{1,0:T(8,128)(4,1)S(1)} %get-tuple-element.168, ...), kind=kLoop, calls=%fused_computation | loop fusion | flops 25165824 | bytes 12593152 | tf_op jit(solution)/shard_map/vmap()/convert_element_type | solution.py:52
  71.1 9.8 %collective-permute-done.2.refs_15_.refs_16_.refs_17_.refs_6_.refs_1_.refs_9_ = bf16[256,1792]{1,0:T(8,128)(2,1)S(1)} collective-permute-done((bf16[256,1792]{1,0:T(8,128)(2,1)S(1)}, bf16[256,1792]{1,0:T(8,128)(2,1)S(1)}, u32[]{:S(2)}, u32[]{:S(2)}) %collective-permute-start.2) | collective-permute-done | bytes 917536 | tf_op jit(solution)/shard_map/ppermute | solution.py:727
  80.9 2.5 collective-permute-done.3.refs_18_.refs_19_.refs_20_.refs_7_.refs_2_.refs_10_
  86.3 5.5 %fusion.10 = (f32[2,1024,128]{2,1,0:T(8,128)}, f32[2,1024,128]{2,1,0:T(8,128)}) fusion(f32[128]{0:T(128)S(1)} %compare_select_fusion, f32[128]{0:T(128)S(1)} %mul.306, f32[2,1024]{1,0:T(2,128)S(1)} %get-tuple-element.158), kind=kLoop, calls=%fused_computation.25 | loop fusion | flops 524288 | bytes 2106368 | tf_op jit(solution)/shard_map/vmap()/mul | solution.py:44
  91.8 4.3 %all-gather.3.cloned.1.call-done.refs_1_.refs_4_ = bf16[2,1024,2048]{2,1,0:T(8,128)(2,1)} async-done(((bf16[2,128,2048]{2,1,0:T(8,128)(2,1)}), bf16[2,1024,2048]{2,1,0:T(8,128)(2,1)}) %all-gather.3.cloned.1.call-update) | async-done | bytes 8388624 | tf_op jit(solution)/shard_map/all_gather | solution.py:905
  96.1 23.2 %attend.1 = (bf16[3,2,1024,256]{3,2,1,0:T(8,128)(2,1)}, bf16[2,1024,256]{2,1,0:T(8,128)(2,1)}, bf16[2,1024,256]{2,1,0:T(8,128)(2,1)}, f32[2,8,1024]{2,1,0:T(8,128)}) custom-call(s32[2,4]{1,0:T(2,128)} %and_select_fusion.1.first_ref, bf16[2,1024,1024]{2,1,0:T(8,128)(2,1)} %get-tuple-element.153.refs_0_.refs_8_, ...), custom_call_target="tpu_custom_call" | custom-call | flops 10000000000 | bytes 10000000 | tf_op jit(solution)/shard_map/attend/pallas_call | solution.py:103
  126.3 17.7 %gelu_units.1 = (bf16[2,1024,1024]{2,1,0:T(8,128)(2,1)}, bf16[2,1024,1024]{2,1,0:T(8,128)(2,1)}) custom-call(s32[1]{0:T(128)} %bitcast.1.first_ref, f32[2,8,1024]{2,1,0:T(8,128)} %get-tuple-element.61.refs_0_.refs_7_, bf16[2,1024,2048]{2,1,0:T(8,128)(2,1)} %all-gather.3.cloned.1.call-done.refs_1_.refs_4_, f32[1,1024]{1,0:T(1,128)} %bitcast.107, ...), custom_call_target="tpu_custom_call" | custom-call | flops 10000000000 | bytes 10000000 | tf_op jit(solution)/shard_map/gelu_units/pallas_call | solution.py:103
  145.1 17.1 %out_sums.1.refs_0_ = bf16[2,1024,2048]{2,1,0:T(8,128)(2,1)} custom-call(s32[1]{0:T(128)} %bitcast.1.first_ref, bf16[2,1024,1024]{2,1,0:T(8,128)(2,1)} %get-tuple-element.62.refs_0_.refs_2_, bf16[2,1024,256]{2,1,0:T(8,128)(2,1)} %get-tuple-element.63.refs_2_.refs_1_.refs_4_, bf16[2,1024,1024]{2,1,0:T(8,128)(2,1)} %get-tuple-element.64.refs_2_, ...), custom_call_target="tpu_custom_call" | custom-call | flops 10000000000 | bytes 10000000 | tf_op jit(solution)/shard_map/out_sums/pallas_call | solution.py:103
  162.2 13.1 %turn.1 = (bf16[2048,2048]{1,0:T(8,128)(2,1)}, bf16[1280,2048]{1,0:T(8,128)(2,1)}) custom-call(s32[1]{0:T(128)} %bitcast.1.first_ref, bf16[2,1024,2048]{2,1,0:T(8,128)(2,1)} %out_sums.1.refs_0_, bf16[2048,2048]{1,0:T(8,128)(2,1)} %bitcast.89, bf16[2048,1024]{1,0:T(8,128)(2,1)} %bitcast.109, bf16[2048,256]{1,0:T(8,128)(2,1)} %bitcast.91), custom_call_target="tpu_custom_call" | custom-call | flops 10000000000 | bytes 10000000 | tf_op jit(solution)/shard_map/turn/pallas_call | solution.py:103
  175.3 3.0 all-gather.5.cloned.1.call-done.refs_6_.refs_1_
  178.4 18.2 %exit_grad.1 = (bf16[1280,256]{1,0:T(8,128)(2,1)}, bf16[1280,256]{1,0:T(8,128)(2,1)}, bf16[1280,512]{1,0:T(8,128)(2,1)}, bf16[1280,512]{1,0:T(8,128)(2,1)}, bf16[1280,512]{1,0:T(8,128)(2,1)}) custom-call(s32[1]{0:T(128)} %bitcast.1.first_ref, bf16[1280,2048]{1,0:T(8,128)(2,1)} %get-tuple-element.67.refs_0_.refs_1_, ...), custom_call_target="tpu_custom_call" | custom-call | flops 10000000000 | bytes 10000000 | tf_op jit(solution)/shard_map/exit_grad/pallas_call | solution.py:103
  199.6 31.4 %attend_back.1 = (bf16[2,1024,768]{2,1,0:T(8,128)(2,1)}, f32[8,256]{1,0:T(8,128)}) custom-call(s32[2,4]{1,0:T(2,128)} %and_select_fusion.1.first_ref, bf16[1280,512]{1,0:T(8,128)(2,1)} %get-tuple-element.68.refs_0_.refs_4_.refs_2_, bf16[3,2,1024,256]{3,2,1,0:T(8,128)(2,1)} %get-tuple-element.69.refs_1_.refs_2_.refs_3_, ...), custom_call_target="tpu_custom_call" | custom-call | flops 10000000000 | bytes 10000000 | tf_op jit(solution)/shard_map/attend_back/pallas_call | solution.py:103
  232.0 3.3 add_halves.1
  235.3 1.6 collective-permute-start.13
  236.9 33.6 %back_rows.1 = (bf16[2,1024,1024]{2,1,0:T(8,128)(2,1)}, bf16[2,1024,2048]{2,1,0:T(8,128)(2,1)}, f32[8,1024]{1,0:T(8,128)}, f32[8,2048]{1,0:T(8,128)}) custom-call(s32[1]{0:T(128)} %bitcast.first_ref, f32[8,256]{1,0:T(8,128)} %get-tuple-element.71.refs_0_, bf16[2,1024,2048]{2,1,0:T(8,128)(2,1)} %all-gather.5.cloned.1.call-done.refs_6_.refs_1_, ...), custom_call_target="tpu_custom_call" | custom-call | flops 10000000000 | bytes 10000000 | tf_op jit(solution)/shard_map/back_rows/pallas_call | solution.py:103
  276.2 15.6 %expand_grad.1 = (bf16[256,1024]{1,0:T(8,128)(2,1)}, bf16[256,1024]{1,0:T(8,128)(2,1)}, bf16[512,1024]{1,0:T(8,128)(2,1)}, bf16[512,1024]{1,0:T(8,128)(2,1)}, bf16[512,1024]{1,0:T(8,128)(2,1)}) custom-call(s32[1]{0:T(128)} %bitcast.1.first_ref, f32[8,2048]{1,0:T(8,128)} %get-tuple-element.73.refs_0_, ...), custom_call_target="tpu_custom_call" | custom-call | flops 10000000000 | bytes 10000000 | tf_op jit(solution)/shard_map/expand_grad/pallas_call | solution.py:103
  294.4 13.8 %heads_grad.1 = (bf16[256,768]{1,0:T(8,128)(2,1)}, bf16[256,768]{1,0:T(8,128)(2,1)}, bf16[512,768]{1,0:T(8,128)(2,1)}, bf16[512,768]{1,0:T(8,128)(2,1)}, bf16[512,768]{1,0:T(8,128)(2,1)}) custom-call(s32[1]{0:T(128)} %bitcast.1.first_ref, bf16[512,1024]{1,0:T(8,128)(2,1)} %get-tuple-element.76.refs_0_.refs_2_, f32[6144]{0:T(1024)} %fusion.33.refs_1_.refs_0_, ...), custom_call_target="tpu_custom_call" | custom-call | flops 10000000000 | bytes 10000000 | tf_op jit(solution)/shard_map/heads_grad/pallas_call | solution.py:103
  314.5 7.5 %adam_sum.4 = (f32[1024,512]{1,0:T(8,128)}, f32[2,1024,512]{2,1,0:T(8,128)}) custom-call(s32[1]{0:T(128)} %bitcast.1.first_ref, bf16[512,768]{1,0:T(8,128)(2,1)} %get-tuple-element.77.refs_0_.refs_2_, bf16[256,768]{1,0:T(8,128)(2,1)} %get-tuple-element.82.refs_1_, bf16[256,768]{1,0:T(8,128)(2,1)} %get-tuple-element.83.refs_2_, f32[2,1024,512]{2,1,0:T(8,128)} %refs_3_.3, ...), custom_call_target="tpu_custom_call" | custom-call | flops 10000000000 | bytes 10000000 | tf_op jit(solution)/shard_map/adam_sum/pallas_call | solution.py:103
  322.0 3.8 adam_sum.5
  325.8 18.1 %collective-permute-done.15.refs_1_ = bf16[256,768]{1,0:T(8,128)(2,1)} collective-permute-done((bf16[256,768]{1,0:T(8,128)(2,1)}, bf16[256,768]{1,0:T(8,128)(2,1)}, u32[]{:S(2)}, u32[]{:S(2)}) %collective-permute-start.15) | collective-permute-done | bytes 393248 | tf_op jit(solution)/shard_map/ppermute | solution.py:727
  350.8 2.6 layer_output.1.refs_0_
  353.4 6.6 %adam_sum.6 = (f32[512,1024]{1,0:T(8,128)}, f32[2,512,1024]{2,1,0:T(8,128)}) custom-call(s32[1]{0:T(128)} %bitcast.1.first_ref, bf16[2,128,2048]{2,1,0:T(8,128)(2,1)} %layer_output.1.refs_0_, f32[2,512,1024]{2,1,0:T(8,128)} %refs_1_.5, bf16[512,1024]{1,0:T(8,128)(2,1)} %get-tuple-element.76.refs_0_.refs_2_, ...), custom_call_target="tpu_custom_call" | custom-call | flops 10000000000 | bytes 10000000 | tf_op jit(solution)/shard_map/adam_sum/pallas_call | solution.py:103
  360.0 4.7 %input_grad.1.refs_1_.refs_0_ = bf16[2,128,2048]{2,1,0:T(8,128)(2,1)} custom-call(s32[1]{0:T(128)} %bitcast.first_ref, f32[2,512,1024]{2,1,0:T(8,128)} %get-tuple-element.115.refs_0_, bf16[2,128,2048]{2,1,0:T(8,128)(2,1)} %refs_1_.6, bf16[2,128,2048]{2,1,0:T(8,128)(2,1)} %refs_2_.3, f32[2,2048]{1,0:T(2,128)} %refs_3_.5, ...), custom_call_target="tpu_custom_call" | custom-call | flops 10000000000 | bytes 10000000 | tf_op jit(solution)/shard_map/input_grad/pallas_call | solution.py:103
  364.8 2.1 collective-permute-start.20
  366.9 2.3 collective-permute-start.21
  370.0 2.8 collective-permute-done.21
  378.0 7.3 %adam_sum.7 = (f32[3,512,256]{2,1,0:T(8,128)}, f32[2,3,512,256]{3,2,1,0:T(8,128)}) custom-call(s32[1]{0:T(128)} %bitcast.1.first_ref, bf16[2,128,2048]{2,1,0:T(8,128)(2,1)} %input_grad.1.refs_1_.refs_0_, f32[2,3,512,256]{3,2,1,0:T(8,128)} %refs_1_.7, bf16[512,768]{1,0:T(8,128)(2,1)} %get-tuple-element.77.refs_0_.refs_2_, bf16[512,768]{1,0:T(8,128)(2,1)} %copy-done.29, ...), custom_call_target="tpu_custom_call" | custom-call | flops 10000000000 | bytes 10000000 | tf_op jit(solution)/shard_map/adam_sum/pallas_call | solution.py:103
  (212 shorter events, 64.1 us)
Async XLA Ops:
  7.2 88.9 %all-gather.3.cloned.1.call-start = ((), (), s32[]{:S(2)}) async-start(), calls=%async_computation.2 | async-start | bytes 9437184 | tf_op jit(solution)/shard_map/all_gather | solution.py:905
  11.2 167.1 %all-gather.5.cloned.1.call-start = ((), (), s32[]{:S(2)}) async-start(), calls=%async_computation.3 | async-start | bytes 9437184 | tf_op jit(solution)/shard_map/all_gather | solution.py:905
  12.4 263.7 %reduce-scatter.3.cloned.1.call-start = ((), (), s32[]{:S(2)}) async-start(), calls=%async_computation.4 | async-start | bytes 9437184 | tf_op jit(solution)/shard_map/reduce_scatter | solution.py:908
  14.9 43.1 %collective-permute-start = (bf16[512,1792]{1,0:T(8,128)(2,1)S(1)}, bf16[512,1792]{1,0:T(8,128)(2,1)}, u32[]{:S(2)}, u32[]{:S(2)}) collective-permute-start(bf16[512,1792]{1,0:T(8,128)(2,1)S(1)} %pad_maximum_fusion.refs_6_.refs_7_.refs_8_.refs_3_), channel_id=1, source_target_pairs={{0,8},{8,0},{16,24},{24,16},{1,9},{9,1},{17,25},{25,17},{2,10},{10... | collective-permute-start | bytes 5505032 | tf_op jit(solution)/shard_map/ppermute | solution.py:727
  17.9 43.2 %collective-permute-start.1 = (bf16[512,1792]{1,0:T(8,128)(2,1)S(1)}, bf16[512,1792]{1,0:T(8,128)(2,1)}, u32[]{:S(2)}, u32[]{:S(2)}) collective-permute-start(bf16[512,1792]{1,0:T(8,128)(2,1)S(1)} %pad_maximum_fusion.refs_6_.refs_7_.refs_8_.refs_3_), channel_id=1, source_target_pairs={{0,16},{8,24},{16,0},{24,8},{1,17},{9,25},{17,1},{25,9},{2,18},{10... | collective-permute-start | bytes 5505032 | tf_op jit(solution)/shard_map/ppermute | solution.py:727
  59.3 21.6 %collective-permute-start.2 = (bf16[256,1792]{1,0:T(8,128)(2,1)S(1)}, bf16[256,1792]{1,0:T(8,128)(2,1)S(1)}, u32[]{:S(2)}, u32[]{:S(2)}) collective-permute-start(bf16[256,1792]{1,0:T(8,128)(2,1)S(1)} %slice.201), channel_id=1, source_target_pairs={{0,16},{8,24},{16,0},{24,8},{1,17},{9,25},{17,1},{25,9},{2,18},{10... | collective-permute-start | bytes 2752520 | tf_op jit(solution)/shard_map/ppermute | solution.py:727
  62.4 21.0 %collective-permute-start.3 = (bf16[256,1792]{1,0:T(8,128)(2,1)S(1)}, bf16[256,1792]{1,0:T(8,128)(2,1)S(1)}, u32[]{:S(2)}, u32[]{:S(2)}) collective-permute-start(bf16[256,1792]{1,0:T(8,128)(2,1)S(1)} %slice.202), channel_id=1, source_target_pairs={{0,8},{8,0},{16,24},{24,16},{1,9},{9,1},{17,25},{25,17},{2,10},{10... | collective-permute-start | bytes 2752520 | tf_op jit(solution)/shard_map/ppermute | solution.py:727
  84.3 35.1 %collective-permute-start.4 = (bf16[1280,512]{1,0:T(8,128)(2,1)}, bf16[1280,512]{1,0:T(8,128)(2,1)S(1)}, u32[]{:S(2)}, u32[]{:S(2)}) collective-permute-start(bf16[1280,512]{1,0:T(8,128)(2,1)} %hold.5.refs_3_.refs_11_), channel_id=1, source_target_pairs={{0,8},{8,0},{16,24},{24,16},{1,9},{9,1},{17,25},{25,17},{2,10},{10... | collective-permute-start | bytes 3932168 | tf_op jit(solution)/shard_map/ppermute | solution.py:727
  85.8 33.6 %collective-permute-start.5 = (bf16[1280,512]{1,0:T(8,128)(2,1)}, bf16[1280,512]{1,0:T(8,128)(2,1)S(1)}, u32[]{:S(2)}, u32[]{:S(2)}) collective-permute-start(bf16[1280,512]{1,0:T(8,128)(2,1)} %hold.5.refs_3_.refs_11_), channel_id=1, source_target_pairs={{0,16},{8,24},{16,0},{24,8},{1,17},{9,25},{17,1},{25,9},{2,18},{10... | collective-permute-start | bytes 3932168 | tf_op jit(solution)/shard_map/ppermute | solution.py:727
  122.1 21.9 %collective-permute-start.6 = (bf16[1280,256]{1,0:T(8,128)(2,1)S(1)}, bf16[1280,256]{1,0:T(8,128)(2,1)S(1)}, u32[]{:S(2)}, u32[]{:S(2)}) collective-permute-start(bf16[1280,256]{1,0:T(8,128)(2,1)S(1)} %slice.169), channel_id=1, source_target_pairs={{0,16},{8,24},{16,0},{24,8},{1,17},{9,25},{17,1},{25,9},{2,18},{10... | collective-permute-start | bytes 1966088 | tf_op jit(solution)/shard_map/ppermute | solution.py:727
  124.7 19.2 %collective-permute-start.7 = (bf16[1280,256]{1,0:T(8,128)(2,1)S(1)}, bf16[1280,256]{1,0:T(8,128)(2,1)S(1)}, u32[]{:S(2)}, u32[]{:S(2)}) collective-permute-start(bf16[1280,256]{1,0:T(8,128)(2,1)S(1)} %slice.170), channel_id=1, source_target_pairs={{0,8},{8,0},{16,24},{24,16},{1,9},{9,1},{17,25},{25,17},{2,10},{10... | collective-permute-start | bytes 1966088 | tf_op jit(solution)/shard_map/ppermute | solution.py:727
  162.2 197.8 %reduce-scatter.5.cloned.1.call-start = ((), (), s32[]{:S(2)}) async-start(), calls=%async_computation.5 | async-start | bytes 9437184 | tf_op jit(solution)/shard_map/reduce_scatter | solution.py:908
  196.6 34.4 %collective-permute-start.11 = (bf16[1280,256]{1,0:T(8,128)(2,1)}, bf16[1280,256]{1,0:T(8,128)(2,1)S(1)}, u32[]{:S(2)}, u32[]{:S(2)}) collective-permute-start(bf16[1280,256]{1,0:T(8,128)(2,1)} %get-tuple-element.86), channel_id=1, source_target_pairs={{0,8},{8,0},{16,24},{24,16},{1,9},{9,1},{17,25},{25,17},{2,10},{10... | collective-permute-start | bytes 1966088 | tf_op jit(solution)/shard_map/ppermute | solution.py:727
  198.1 32.9 %collective-permute-start.12 = (bf16[1280,256]{1,0:T(8,128)(2,1)}, bf16[1280,256]{1,0:T(8,128)(2,1)S(1)}, u32[]{:S(2)}, u32[]{:S(2)}) collective-permute-start(bf16[1280,256]{1,0:T(8,128)(2,1)} %get-tuple-element.87), channel_id=1, source_target_pairs={{0,16},{8,24},{16,0},{24,8},{1,17},{9,25},{17,1},{25,9},{2,18},{10... | collective-permute-start | bytes 1966088 | tf_op jit(solution)/shard_map/ppermute | solution.py:727
  235.3 35.2 %collective-permute-start.13 = (bf16[1280,512]{1,0:T(8,128)(2,1)}, bf16[1280,512]{1,0:T(8,128)(2,1)S(1)}, u32[]{:S(2)}, u32[]{:S(2)}) collective-permute-start(bf16[1280,512]{1,0:T(8,128)(2,1)} %get-tuple-element.88), channel_id=1, source_target_pairs={{0,8},{8,0},{16,24},{24,16},{1,9},{9,1},{17,25},{25,17},{2,10},{10... | collective-permute-start | bytes 3932168 | tf_op jit(solution)/shard_map/ppermute | solution.py:727
  236.9 33.6 %collective-permute-start.14 = (bf16[1280,512]{1,0:T(8,128)(2,1)}, bf16[1280,512]{1,0:T(8,128)(2,1)S(1)}, u32[]{:S(2)}, u32[]{:S(2)}) collective-permute-start(bf16[1280,512]{1,0:T(8,128)(2,1)} %get-tuple-element.89), channel_id=1, source_target_pairs={{0,16},{8,24},{16,0},{24,8},{1,17},{9,25},{17,1},{25,9},{2,18},{10... | collective-permute-start | bytes 3932168 | tf_op jit(solution)/shard_map/ppermute | solution.py:727
  274.3 1.3 collective-permute-start.8
  291.7 18.0 %collective-permute-start.9 = (bf16[256,1024]{1,0:T(8,128)(2,1)}, bf16[256,1024]{1,0:T(8,128)(2,1)S(1)}, u32[]{:S(2)}, u32[]{:S(2)}) collective-permute-start(bf16[256,1024]{1,0:T(8,128)(2,1)} %get-tuple-element.80), channel_id=1, source_target_pairs={{0,8},{8,0},{16,24},{24,16},{1,9},{9,1},{17,25},{25,17},{2,10},{10... | collective-permute-start | bytes 1572872 | tf_op jit(solution)/shard_map/ppermute | solution.py:727
  293.0 17.7 %collective-permute-start.10 = (bf16[256,1024]{1,0:T(8,128)(2,1)}, bf16[256,1024]{1,0:T(8,128)(2,1)S(1)}, u32[]{:S(2)}, u32[]{:S(2)}) collective-permute-start(bf16[256,1024]{1,0:T(8,128)(2,1)} %get-tuple-element.81), channel_id=1, source_target_pairs={{0,16},{8,24},{16,0},{24,8},{1,17},{9,25},{17,1},{25,9},{2,18},{10... | collective-permute-start | bytes 1572872 | tf_op jit(solution)/shard_map/ppermute | solution.py:727
  310.0 43.4 %collective-permute-start.18 = (bf16[512,1024]{1,0:T(8,128)(2,1)S(1)}, bf16[512,1024]{1,0:T(8,128)(2,1)}, u32[]{:S(2)}, u32[]{:S(2)}) collective-permute-start(bf16[512,1024]{1,0:T(8,128)(2,1)S(1)} %pad_maximum_fusion.5), channel_id=1, source_target_pairs={{0,16},{8,24},{16,0},{24,8},{1,17},{9,25},{17,1},{25,9},{2,18},{10... | collective-permute-start | bytes 3145736 | tf_op jit(solution)/shard_map/ppermute | solution.py:727
  311.0 42.4 %collective-permute-start.17 = (bf16[512,1024]{1,0:T(8,128)(2,1)S(1)}, bf16[512,1024]{1,0:T(8,128)(2,1)}, u32[]{:S(2)}, u32[]{:S(2)}) collective-permute-start(bf16[512,1024]{1,0:T(8,128)(2,1)S(1)} %pad_maximum_fusion.4), channel_id=1, source_target_pairs={{0,8},{8,0},{16,24},{24,16},{1,9},{9,1},{17,25},{25,17},{2,10},{10... | collective-permute-start | bytes 3145736 | tf_op jit(solution)/shard_map/ppermute | solution.py:727
  311.9 32.0 %collective-permute-start.15 = (bf16[256,768]{1,0:T(8,128)(2,1)}, bf16[256,768]{1,0:T(8,128)(2,1)}, u32[]{:S(2)}, u32[]{:S(2)}) collective-permute-start(bf16[256,768]{1,0:T(8,128)(2,1)} %get-tuple-element.82.refs_1_), channel_id=1, source_target_pairs={{0,8},{8,0},{16,24},{24,16},{1,9},{9,1},{17,25},{25,17},{2,10},{10... | collective-permute-start | bytes 1179656 | tf_op jit(solution)/shard_map/ppermute | solution.py:727
  313.1 34.3 %collective-permute-start.16 = (bf16[256,768]{1,0:T(8,128)(2,1)}, bf16[256,768]{1,0:T(8,128)(2,1)}, u32[]{:S(2)}, u32[]{:S(2)}) collective-permute-start(bf16[256,768]{1,0:T(8,128)(2,1)} %get-tuple-element.83.refs_2_), channel_id=1, source_target_pairs={{0,16},{8,24},{16,0},{24,8},{1,17},{9,25},{17,1},{25,9},{2,18},{10... | collective-permute-start | bytes 1179656 | tf_op jit(solution)/shard_map/ppermute | solution.py:727
  322.0 21.9 %copy-start.16 = (bf16[512,768]{1,0:T(8,128)(2,1)S(1)}, bf16[512,768]{1,0:T(8,128)(2,1)}, u32[]{:S(2)}) copy-start(bf16[512,768]{1,0:T(8,128)(2,1)} %get-tuple-element.98) | copy-start | bytes 2359300
  346.0 31.1 %collective-permute-start.26 = (bf16[512,768]{1,0:T(8,128)(2,1)}, bf16[512,768]{1,0:T(8,128)(2,1)}, u32[]{:S(2)}, u32[]{:S(2)}) collective-permute-start(bf16[512,768]{1,0:T(8,128)(2,1)} %pad_maximum_fusion.7), channel_id=1, source_target_pairs={{0,16},{8,24},{16,0},{24,8},{1,17},{9,25},{17,1},{25,9},{2,18},{10... | collective-permute-start | bytes 2359304 | tf_op jit(solution)/shard_map/ppermute | solution.py:727
  349.5 27.6 %collective-permute-start.25 = (bf16[512,768]{1,0:T(8,128)(2,1)}, bf16[512,768]{1,0:T(8,128)(2,1)S(1)}, u32[]{:S(2)}, u32[]{:S(2)}) collective-permute-start(bf16[512,768]{1,0:T(8,128)(2,1)} %pad_maximum_fusion.6), channel_id=1, source_target_pairs={{0,8},{8,0},{16,24},{24,16},{1,9},{9,1},{17,25},{25,17},{2,10},{10... | collective-permute-start | bytes 2359304 | tf_op jit(solution)/shard_map/ppermute | solution.py:727
  364.7 5.3 %collective-permute-start.19 = (f32[6144]{0:T(1024)}, f32[6144]{0:T(1024)S(1)}, u32[]{:S(2)}, u32[]{:S(2)}) collective-permute-start(f32[6144]{0:T(1024)} %hold.9), channel_id=1, source_target_pairs={{0,2},{1,3},{2,0},{3,1},{4,6},{5,7},{6,4},{7,5},{8,10},{9,11},{10,... | collective-permute-start | bytes 73736 | tf_op jit(solution)/shard_map/ppermute | solution.py:843
  364.8 5.2 %collective-permute-start.20 = (f32[6144]{0:T(1024)}, f32[6144]{0:T(1024)S(1)}, u32[]{:S(2)}, u32[]{:S(2)}) collective-permute-start(f32[6144]{0:T(1024)} %hold.9), channel_id=1, source_target_pairs={{0,4},{1,5},{2,6},{3,7},{4,0},{5,1},{6,2},{7,3},{8,12},{9,13},{10,... | collective-permute-start | bytes 73736 | tf_op jit(solution)/shard_map/ppermute | solution.py:843
  366.9 5.8 %collective-permute-start.21 = (f32[6144]{0:T(1024)}, f32[6144]{0:T(1024)S(1)}, u32[]{:S(2)}, u32[]{:S(2)}) collective-permute-start(f32[6144]{0:T(1024)} %hold.9), channel_id=1, source_target_pairs={{0,6},{1,7},{2,4},{3,5},{4,2},{5,3},{6,0},{7,1},{8,14},{9,15},{10,... | collective-permute-start | bytes 73736 | tf_op jit(solution)/shard_map/ppermute | solution.py:843
  373.5 11.8 %collective-permute-start.22 = (f32[7936]{0:T(1024)S(1)}, f32[7936]{0:T(1024)S(1)}, u32[]{:S(2)}, u32[]{:S(2)}) collective-permute-start(f32[7936]{0:T(1024)S(1)} %pad_maximum_fusion.8), channel_id=1, source_target_pairs={{0,8},{8,0},{16,24},{24,16},{1,9},{9,1},{17,25},{25,17},{2,10},{10... | collective-permute-start | bytes 95240 | tf_op jit(solution)/shard_map/ppermute | solution.py:843
  374.3 11.0 %collective-permute-start.23 = (f32[7936]{0:T(1024)S(1)}, f32[7936]{0:T(1024)S(1)}, u32[]{:S(2)}, u32[]{:S(2)}) collective-permute-start(f32[7936]{0:T(1024)S(1)} %pad_maximum_fusion.8), channel_id=1, source_target_pairs={{0,16},{8,24},{16,0},{24,8},{1,17},{9,25},{17,1},{25,9},{2,18},{10... | collective-permute-start | bytes 95240 | tf_op jit(solution)/shard_map/ppermute | solution.py:843
  375.7 9.6 %collective-permute-start.24 = (f32[7936]{0:T(1024)S(1)}, f32[7936]{0:T(1024)S(1)}, u32[]{:S(2)}, u32[]{:S(2)}) collective-permute-start(f32[7936]{0:T(1024)S(1)} %pad_maximum_fusion.8), channel_id=1, source_target_pairs={{0,24},{8,16},{16,8},{24,0},{1,25},{9,17},{17,9},{25,1},{2,26},{10... | collective-permute-start | bytes 95240 | tf_op jit(solution)/shard_map/ppermute | solution.py:843
  (31 other events, 159.2 us)
Sparse Core Ops, SparseCore 0:
  11.3 84.7 all-gather.2
  97.7 80.5 all-gather.4
  180.7 88.1 reduce-scatter.2
  272.2 87.7 reduce-scatter.4
